TPU v7x, 32 devices: a whole 2x2x4 slice. The times are simulated.
32 devices in a mesh: dom: 16 (over z, y, x), dim: 2 (over core).
Axes of the slice: x: 2, y: 2, z: 4, core: 2. Of those that a mesh axis runs over, the one named last changes fastest.
Arguments:
- ent_re: float32 [200, 8192], P('dim', 'dom'), may hold values from -8 to 8
- ent_im: float32 [200, 8192], P('dim', 'dom'), may hold values from -8 to 8
- ent_acc: float32 [8192], P('dom'), may hold values from 0.001 to 0.1
- rel_re: float32 [200, 4096], P('dim'), may hold values from -2.5 to 2.5
- rel_im: float32 [200, 4096], P('dim'), may hold values from -2.5 to 2.5
- rel_acc: float32 [4096], replicated, may hold values from 0.001 to 0.1
- lhs_rows: int32 [32, 128], P('dom'), may hold values from 0 to 511
- rhs_rows: int32 [32, 128], P('dom'), may hold values from 0 to 511
- rel_ids: int32 [32, 128], P('dom'), may hold values from 0 to 4095
- neg_rows: int32 [32, 1000], P('dom'), may hold values from 0 to 511
- bucket_step: int32 [32], P('dom'), may hold values from 0 to 4
Outputs:
- new_ent_re: float32 [200, 8192], P('dim', 'dom')
- new_ent_im: float32 [200, 8192], P('dim', 'dom')
- new_ent_acc: float32 [8192], P('dom')
- new_rel_re: float32 [200, 4096], P('dim')
- new_rel_im: float32 [200, 4096], P('dim')
- new_rel_acc: float32 [4096], replicated
Inputs may be any that keep to these rules, and one draw needn't show every extreme that they name: bucket_step equal to 4 marks an empty slot.
All inputs are finite; a program needn't handle non-finite values.
Results may differ from a plain program's by a relative error of at most 0.0003.
Values sent between devices are 32-bit elements; how exact they have to be, the bound alone decides.
A program may use at most 64 MiB of HBM per device.

v0:
```python
import jax
import jax.numpy as jnp
from jax import lax
from jax.sharding import PartitionSpec as P

D = 400
STEPS = 4


learn_rate = 0.1


def from_behind(block, axis, distance):
    devices = range(lax.axis_size(axis))
    route = [((i - distance) % len(devices), i) for i in devices]
    return lax.ppermute(block, axis, route)


def score_weights(pos, neg, live):
    top = jnp.maximum(jnp.max(neg, -1), pos)
    e_pos = jnp.exp(pos - top)
    e_neg = jnp.exp(neg - top[..., None])
    denom = e_pos + jnp.sum(e_neg, -1)
    w_pos = (e_pos / denom - 1.0) * live[:, None]
    w_neg = e_neg / denom[..., None] * live[:, None, None]
    return (w_pos, w_neg)


def column_sum(values, indices, count):
    full = values.shape[0]
    empty = jnp.zeros((full, count), jnp.float32)
    return empty.at[:, indices.reshape(-1)].add(values.reshape(full, -1))


def complex_product(left, right, half):
    l_re, l_im = (left[:half], left[half:])
    r_re, r_im = (right[:half], right[half:])
    return jnp.concatenate([l_re * r_re - l_im * r_im, l_re * r_im + l_im * r_re], 0)


def per_device(
    ent_re,
    ent_im,
    ent_acc,
    rel_re,
    rel_im,
    rel_acc,
    lhs_rows,
    rhs_rows,
    rel_ids,
    neg_rows,
    bucket_step,
):
    width = ent_re.shape[0]
    rows = ent_re.shape[1]
    hp = lax.Precision.HIGHEST
    own_block = jnp.concatenate([ent_re, ent_im], 0)
    relation = jnp.concatenate([rel_re, rel_im], 0)
    live = (bucket_step < STEPS).astype(jnp.float32)
    stepc = jnp.minimum(bucket_step, STEPS - 1)
    groups = lhs_rows.shape[0]
    per_edge = lhs_rows.shape[1]
    full = 2 * width
    rel_cols = relation[:, rel_ids]
    tails = jnp.zeros((full, groups, per_edge), jnp.float32)
    negatives = jnp.zeros((full, groups, neg_rows.shape[1]), jnp.float32)
    block = own_block
    for step in range(STEPS):
        if step > 0:
            block = from_behind(block, "dom", 1)
        chosen = (bucket_step == step)[None, :, None]
        tails = jnp.where(chosen, block[:, rhs_rows], tails)
        negatives = jnp.where(chosen, block[:, neg_rows], negatives)
    head = own_block[:, lhs_rows]
    h_re, h_im = (head[:width], head[width:])
    r_re, r_im = (rel_cols[:width], rel_cols[width:])
    query = complex_product(head, rel_cols, width)
    pos_part = jnp.sum(query * tails, 0)
    neg_part = jnp.einsum("kce,kcn->cen", query, negatives, precision=hp)
    pos, neg = lax.psum((pos_part, neg_part), "dim")
    w_pos, w_neg = score_weights(pos, neg, live)
    grad_query = w_pos[None] * tails + jnp.einsum("cen,kcn->kce", w_neg, negatives, precision=hp)
    grad_tail = w_pos[None] * query
    grad_negative = jnp.einsum("cen,kce->kcn", w_neg, query, precision=hp)
    gq_re, gq_im = (grad_query[:width], grad_query[width:])
    grad_head = jnp.concatenate([gq_re * r_re + gq_im * r_im, gq_im * r_re - gq_re * r_im], 0)
    grad_rel = jnp.concatenate([gq_re * h_re + gq_im * h_im, gq_im * h_re - gq_re * h_im], 0)
    lhs_grad = column_sum(grad_head, lhs_rows, rows)
    tail_ids = rhs_rows + (stepc * rows)[:, None]
    neg_ids = neg_rows + (stepc * rows)[:, None]
    step_grads = column_sum(grad_tail, tail_ids, rows * STEPS)
    step_grads = step_grads + column_sum(grad_negative, neg_ids, rows * STEPS)
    step_grads = step_grads.reshape(full, STEPS, rows)
    carried = step_grads[:, STEPS - 1]
    for turn in range(1, STEPS):
        carried = from_behind(carried, "dom", -1) + step_grads[:, STEPS - 1 - turn]
    total = lhs_grad + carried
    local_rel = column_sum(grad_rel, rel_ids, relation.shape[1])
    rel_total = lax.psum(local_rel, "dom")
    ent_sq, rel_sq = lax.psum((jnp.sum(total * total, 0), jnp.sum(rel_total * rel_total, 0)), "dim")
    new_ent_acc = ent_acc + ent_sq / D
    new_rel_acc = rel_acc + rel_sq / D
    ent_scale = learn_rate / jnp.sqrt(new_ent_acc)[None, :]
    rel_scale = learn_rate / jnp.sqrt(new_rel_acc)[None, :]
    new_ent = own_block - ent_scale * total
    new_rel = relation - rel_scale * rel_total
    return (
        new_ent[:width],
        new_ent[width:],
        new_ent_acc,
        new_rel[:width],
        new_rel[width:],
        new_rel_acc,
    )


def solution(mesh):
    return jax.shard_map(
        per_device,
        mesh=mesh,
        in_specs=(
            P("dim", "dom"),
            P("dim", "dom"),
            P("dom"),
            P("dim", None),
            P("dim", None),
            P(),
            P("dom", None),
            P("dom", None),
            P("dom", None),
            P("dom", None),
            P("dom"),
        ),
        out_specs=(P("dim", "dom"), P("dim", "dom"), P("dom"), P("dim", None), P("dim", None), P()),
        check_vma=False,
    )
```

profile of v0, /device:TPU:0, one launch (start us, length us, event | category | flops | bytes accessed | tf_op | source)
XLA Modules:
  0.0 343.3 jit_solution(5891365343984814943)
XLA Ops:
  8.3 1.1 copy.30
  10.3 3.0 collective-permute-start
  17.3 6.8 %gather_fusion.9 = f32[2000,200]{1,0:T(8,128)S(1)} fusion(f32[200,512]{0,1:T(8,128)S(1)} %pad_maximum_fusion.1, s32[2048]{0:T(1024)S(1)} %pad_clamp_fusion), kind=kCustom, calls=%fused_computation.9 | custom fusion | bytes 3208000 | tf_op jit(solution)/shard_map/gather | solution.py:73
  24.1 1.7 copy.45
  25.9 3.0 copy.33
  28.9 1.8 copy.34
  30.7 1.5 collective-permute-start.1
  32.3 5.3 %pad_maximum_fusion = f32[200,4096]{0,1:T(8,128)} fusion(f32[100,4096]{0,1:T(8,128)} %copy.34, f32[100,4096]{0,1:T(8,128)} %copy.33), kind=kLoop, calls=%fused_computation.14 | loop fusion | flops 819200 | bytes 6553600 | tf_op jit(solution)/shard_map/concatenate | solution.py:58
  37.6 3.2 gather_fusion.1
  40.9 6.8 %collective-permute-done.1 = f32[200,512]{0,1:T(8,128)S(1)} collective-permute-done((f32[200,512]{0,1:T(8,128)S(1)}, f32[200,512]{0,1:T(8,128)S(1)}, u32[]{:S(2)}, u32[]{:S(2)}) %collective-permute-start.1) | collective-permute-done | bytes 409632 | tf_op jit(solution)/shard_map/ppermute | solution.py:16
  49.2 8.5 %gather_fusion.8 = f32[2000,200]{1,0:T(8,128)} fusion(f32[200,512]{0,1:T(8,128)S(1)} %collective-permute-done, s32[2048]{0:T(1024)S(1)} %pad_clamp_fusion), kind=kCustom, calls=%fused_computation.8 | custom fusion | bytes 3208000 | tf_op jit(solution)/shard_map/gather | solution.py:73
  57.7 2.8 copy.46
  60.5 8.5 %gather_fusion.7 = f32[2000,200]{1,0:T(8,128)} fusion(f32[200,512]{0,1:T(8,128)S(1)} %collective-permute-done.1, s32[2048]{0:T(1024)S(1)} %pad_clamp_fusion), kind=kCustom, calls=%fused_computation.7 | custom fusion | bytes 3208000 | tf_op jit(solution)/shard_map/gather | solution.py:73
  69.0 2.8 copy.47
  71.8 8.5 %gather_fusion.6 = f32[2000,200]{1,0:T(8,128)} fusion(f32[200,512]{0,1:T(8,128)S(1)} %collective-permute-done.2, s32[2048]{0:T(1024)S(1)} %pad_clamp_fusion), kind=kCustom, calls=%fused_computation.6 | custom fusion | bytes 3208000 | tf_op jit(solution)/shard_map/gather | solution.py:73
  80.3 2.8 copy.48
  83.1 3.7 %select_select_fusion = f32[2,1000,200]{1,2,0:T(8,128)S(1)} fusion(f32[2,1000,200]{1,2,0:T(8,128)} %copy.48, f32[2,1000,200]{1,2,0:T(8,128)} %copy.47, f32[2,1000,200]{1,2,0:T(8,128)} %copy.46, f32[2,1000,200]{1,2,0:T(8,128)} %copy.45, pred[2]{0:T(512)(128)(4,1)S(1)} %get-tuple-element.44, pred[2]{0:T(512)(128)(4,1)S(1)} %get-tuple-element.46, ...), kind=kLoop, calls=%fused_computation.23 | loop fusion | flops 1600000 | bytes 8000008 | tf_op jit(solution)/shard_map/jit(_where)/select_n | solution.py:73
  86.8 1.2 copy-done.1
  87.9 4.4 %fusion.4 = f32[2,128,1000]{1,2,0:T(8,128)} fusion(f32[2,1000,200]{1,2,0:T(8,128)S(1)} %select_select_fusion, f32[100,2,128]{2,0,1:T(8,128)S(1)} %get-tuple-element.35, f32[100,2,128]{2,0,1:T(8,128)S(1)} %get-tuple-element.34), kind=kOutput, calls=%fused_computation.21 | convolution fusion | flops 614451200 | bytes 2828800 | tf_op jit(solution)/shard_map/kce,kcn->cen/dot_general | solution.py:79
  101.6 1.3 fusion.21
  102.9 2.5 psum.35
  105.4 8.0 %all-reduce.4.cloned.1.call-done = f32[2,128,1000]{1,2,0:T(8,128)} async-done(((f32[2,128,1000]{1,2,0:T(8,128)}), f32[2,128,1000]{1,2,0:T(8,128)}) %all-reduce.4.cloned.1.call-update) | async-done | bytes 1024016 | tf_op jit(solution)/shard_map/psum | solution.py:80
  113.4 1.4 reduce_max.9
  114.8 1.4 fusion.16
  116.2 3.0 fusion.9
  120.2 4.1 %scatter_custom_fusion.3 = f32[200,4096]{0,1:T(8,128)} fusion(s32[256]{0:T(256)S(1)} %bitcast.120, f32[256,200]{1,0:T(8,128)S(1)} %copy.57, f32[]{:T(128)} %constant.14.clone.1), kind=kCustom, calls=%fused_computation.17 | custom fusion | flops 51200 | bytes 3276804 | tf_op jit(solution)/shard_map/scatter-add | solution.py:32
  126.1 1.6 convolution_bitcast_fusion
  127.8 1.3 copy.52
  129.0 1.8 reshape.264
  130.8 1.8 copy.53
  132.6 12.4 %scatter_custom_fusion.1 = f32[200,2048]{0,1:T(8,128)} fusion(s32[2000]{0:T(1024)S(1)} %bitcast.113, f32[2000,200]{1,0:T(8,128)} %copy.53, f32[]{:T(128)} %constant.14.clone.1), kind=kCustom, calls=%fused_computation.27 | custom fusion | flops 400000 | bytes 1638912 | tf_op jit(solution)/shard_map/scatter-add | solution.py:32
  145.0 3.7 %scatter_custom_fusion = f32[200,2048]{0,1:T(8,128)} fusion(s32[256]{0:T(256)S(1)} %bitcast.119, f32[256,200]{1,0:T(8,128)} %copy.51, f32[]{:T(128)} %constant.14.clone.1), kind=kCustom, calls=%fused_computation.29 | custom fusion | flops 51200 | bytes 1638912 | tf_op jit(solution)/shard_map/scatter-add | solution.py:32
  148.7 2.6 add.158
  151.5 5.4 %collective-permute-start.3 = (f32[200,512]{0,1:T(8,128)S(1)}, f32[200,512]{0,1:T(8,128)S(1)}, u32[]{:S(2)}, u32[]{:S(2)}) collective-permute-start(f32[200,512]{0,1:T(8,128)S(1)} %slice_bitcast_fusion.3), channel_id=1, source_target_pairs={{2,0},{4,2},{6,4},{8,6},{10,8},{12,10},{14,12},{16,14},{18,16},{20... | collective-permute-start | bytes 1228808 | tf_op jit(solution)/shard_map/ppermute | solution.py:16
  156.8 19.5 %collective-permute-done.3 = f32[200,512]{0,1:T(8,128)S(1)} collective-permute-done((f32[200,512]{0,1:T(8,128)S(1)}, f32[200,512]{0,1:T(8,128)S(1)}, u32[]{:S(2)}, u32[]{:S(2)}) %collective-permute-start.3) | collective-permute-done | bytes 409632 | tf_op jit(solution)/shard_map/ppermute | solution.py:16
  176.4 6.1 %collective-permute-start.4 = (f32[200,512]{0,1:T(8,128)S(1)}, f32[200,512]{0,1:T(8,128)S(1)}, u32[]{:S(2)}, u32[]{:S(2)}) collective-permute-start(f32[200,512]{0,1:T(8,128)S(1)} %fusion.19), channel_id=1, source_target_pairs={{2,0},{4,2},{6,4},{8,6},{10,8},{12,10},{14,12},{16,14},{18,16},{20... | collective-permute-start | bytes 1228808 | tf_op jit(solution)/shard_map/ppermute | solution.py:16
  182.5 18.0 %collective-permute-done.4 = f32[200,512]{0,1:T(8,128)S(1)} collective-permute-done((f32[200,512]{0,1:T(8,128)S(1)}, f32[200,512]{0,1:T(8,128)S(1)}, u32[]{:S(2)}, u32[]{:S(2)}) %collective-permute-start.4) | collective-permute-done | bytes 409632 | tf_op jit(solution)/shard_map/ppermute | solution.py:16
  201.4 6.1 %collective-permute-start.5 = (f32[200,512]{0,1:T(8,128)}, f32[200,512]{0,1:T(8,128)}, u32[]{:S(2)}, u32[]{:S(2)}) collective-permute-start(f32[200,512]{0,1:T(8,128)} %fusion.18), channel_id=1, source_target_pairs={{2,0},{4,2},{6,4},{8,6},{10,8},{12,10},{14,12},{16,14},{18,16},{20... | collective-permute-start | bytes 1228808 | tf_op jit(solution)/shard_map/ppermute | solution.py:16
  207.7 13.1 %collective-permute-done.5 = f32[200,512]{0,1:T(8,128)} collective-permute-done((f32[200,512]{0,1:T(8,128)}, f32[200,512]{0,1:T(8,128)}, u32[]{:S(2)}, u32[]{:S(2)}) %collective-permute-start.5) | collective-permute-done | bytes 409632 | tf_op jit(solution)/shard_map/ppermute | solution.py:16
  220.8 1.1 fusion.17
  221.9 2.4 scatter_fusion
  224.5 92.0 %all-reduce.6.cloned.1.call-done = f32[200,4096]{0,1:T(8,128)} async-done(((f32[200,4096]{0,1:T(8,128)}), f32[200,4096]{0,1:T(8,128)}) %all-reduce.6.cloned.1.call-update) | async-done | bytes 3276816 | tf_op jit(solution)/shard_map/psum | solution.py:99
  316.5 2.8 multiply_reduce_fusion
  319.3 3.5 %all-reduce = (f32[512]{0:T(512)S(1)}, f32[4096]{0:T(1024)S(1)}) all-reduce(f32[512]{0:T(512)S(1)} %multiply_reduce_fusion.1, f32[4096]{0:T(1024)S(1)} %multiply_reduce_fusion), channel_id=1, replica_groups=mesh['dom'=16,'dim'=2] {'dim'}, use_global_device_ids=true, to_apply=%region_9.10 | all-reduce | flops 4608 | bytes 36864 | tf_op jit(solution)/shard_map/psum | solution.py:100
  325.3 3.7 %multiply_subtract_fusion = f32[200,4096]{0,1:T(8,128)S(1)} fusion(f32[200,4096]{0,1:T(8,128)} %all-reduce.6.cloned.1.call-done, f32[4096]{0:T(1024)S(1)} %get-tuple-element.20, f32[100,4096]{0,1:T(8,128)} %copy.34, f32[100,4096]{0,1:T(8,128)S(1)} %copy-done), kind=kLoop, calls=%fused_computation.15 | loop fusion | flops 2457600 | bytes 9846784 | tf_op jit(solution)/shard_map/sub | solution.py:106
  329.0 2.0 fusion.28
  331.0 2.9 copy.61
  334.7 1.8 copy.60
  (96 shorter events, 24.2 us)
Async XLA Ops:
  7.2 106.3 %all-reduce.4.cloned.1.call-start = ((), (), s32[]{:S(2)}) async-start(), calls=%async_computation | async-start | bytes 2048000 | tf_op jit(solution)/shard_map/psum | solution.py:80
  9.4 0.7 copy-start.4
  10.3 20.5 %collective-permute-start = (f32[200,512]{0,1:T(8,128)S(1)}, f32[200,512]{0,1:T(8,128)S(1)}, u32[]{:S(2)}, u32[]{:S(2)}) collective-permute-start(f32[200,512]{0,1:T(8,128)S(1)} %pad_maximum_fusion.1), channel_id=1, source_target_pairs={{30,0},{0,2},{2,4},{4,6},{6,8},{8,10},{10,12},{12,14},{14,16},{16,... | collective-permute-start | bytes 1228808 | tf_op jit(solution)/shard_map/ppermute | solution.py:16
  25.9 3.0 copy-start.7
  28.8 1.8 copy-start.12
  30.7 17.0 %collective-permute-start.1 = (f32[200,512]{0,1:T(8,128)S(1)}, f32[200,512]{0,1:T(8,128)S(1)}, u32[]{:S(2)}, u32[]{:S(2)}) collective-permute-start(f32[200,512]{0,1:T(8,128)S(1)} %collective-permute-done), channel_id=1, source_target_pairs={{30,0},{0,2},{2,4},{4,6},{6,8},{8,10},{10,12},{12,14},{14,16},{16,... | collective-permute-start | bytes 1228808 | tf_op jit(solution)/shard_map/ppermute | solution.py:16
  37.6 10.2 %copy-start.6 = (f32[2,128,200]{1,2,0:T(8,128)S(1)}, f32[2,128,200]{1,2,0:T(8,128)}, u32[]{:S(2)}) copy-start(f32[2,128,200]{1,2,0:T(8,128)} %copy.32) | copy-start | bytes 614404
  37.6 11.6 %copy-start.16 = (s32[2]{0:T(128)S(1)}, s32[2]{0:T(128)}, u32[]{:S(2)}) copy-start(s32[2]{0:T(128)} %param.21) | copy-start | bytes 28
  47.8 24.0 %collective-permute-start.2 = (f32[200,512]{0,1:T(8,128)S(1)}, f32[200,512]{0,1:T(8,128)S(1)}, u32[]{:S(2)}, u32[]{:S(2)}) collective-permute-start(f32[200,512]{0,1:T(8,128)S(1)} %collective-permute-done.1), channel_id=1, source_target_pairs={{30,0},{0,2},{2,4},{4,6},{6,8},{8,10},{10,12},{12,14},{14,16},{16,... | collective-permute-start | bytes 1228808 | tf_op jit(solution)/shard_map/ppermute | solution.py:16
  86.8 1.2 copy-start.1
  87.9 4.6 %copy-start.15 = (s32[2,128]{1,0:T(2,128)S(1)}, s32[2,128]{1,0:T(2,128)}, u32[]{:S(2)}) copy-start(s32[2,128]{1,0:T(2,128)} %param.18) | copy-start | bytes 3076
  92.3 224.1 %all-reduce.6.cloned.1.call-start = ((), (), s32[]{:S(2)}) async-start(), calls=%async_computation.1 | async-start | bytes 8388608 | tf_op jit(solution)/shard_map/psum | solution.py:99
  101.5 14.8 %copy-start.2 = (f32[2,1000,200]{1,2,0:T(8,128)S(1)}, f32[2,1000,200]{1,2,0:T(8,128)}, u32[]{:S(2)}) copy-start(f32[2,1000,200]{1,2,0:T(8,128)} %copy-done.1) | copy-start | bytes 4800004
  124.3 0.9 copy-start.9
  124.3 0.9 copy-start.10
  124.3 1.8 copy-start.3
  151.4 56.1 %copy-start.13 = (s32[2,128]{1,0:T(2,128)S(1)}, s32[2,128]{1,0:T(2,128)}, u32[]{:S(2)}) copy-start(s32[2,128]{1,0:T(2,128)} %param.17) | copy-start | bytes 3076
  151.4 56.1 %copy-start.8 = (f32[2,25,8,128]{3,2,1,0:T(8,128)S(1)}, f32[2,25,8,128]{3,2,1,0:T(8,128)}, u32[]{:S(2)}) copy-start(f32[2,25,8,128]{3,2,1,0:T(8,128)} %get-tuple-element.49) | copy-start | bytes 614404
  151.5 24.9 %collective-permute-start.3 = (f32[200,512]{0,1:T(8,128)S(1)}, f32[200,512]{0,1:T(8,128)S(1)}, u32[]{:S(2)}, u32[]{:S(2)}) collective-permute-start(f32[200,512]{0,1:T(8,128)S(1)} %slice_bitcast_fusion.3), channel_id=1, source_target_pairs={{2,0},{4,2},{6,4},{8,6},{10,8},{12,10},{14,12},{16,14},{18,16},{20... | collective-permute-start | bytes 1228808 | tf_op jit(solution)/shard_map/ppermute | solution.py:16
  176.4 24.1 %collective-permute-start.4 = (f32[200,512]{0,1:T(8,128)S(1)}, f32[200,512]{0,1:T(8,128)S(1)}, u32[]{:S(2)}, u32[]{:S(2)}) collective-permute-start(f32[200,512]{0,1:T(8,128)S(1)} %fusion.19), channel_id=1, source_target_pairs={{2,0},{4,2},{6,4},{8,6},{10,8},{12,10},{14,12},{16,14},{18,16},{20... | collective-permute-start | bytes 1228808 | tf_op jit(solution)/shard_map/ppermute | solution.py:16
  201.4 19.3 %collective-permute-start.5 = (f32[200,512]{0,1:T(8,128)}, f32[200,512]{0,1:T(8,128)}, u32[]{:S(2)}, u32[]{:S(2)}) collective-permute-start(f32[200,512]{0,1:T(8,128)} %fusion.18), channel_id=1, source_target_pairs={{2,0},{4,2},{6,4},{8,6},{10,8},{12,10},{14,12},{16,14},{18,16},{20... | collective-permute-start | bytes 1228808 | tf_op jit(solution)/shard_map/ppermute | solution.py:16
  224.4 98.4 %copy-start.14 = (f32[512]{0:T(512)S(1)}, f32[512]{0:T(512)}, u32[]{:S(2)}) copy-start(f32[512]{0:T(512)} %param.13) | copy-start | bytes 6148
  224.5 99.0 %copy-start.5 = (f32[100,512]{0,1:T(8,128)S(1)}, f32[100,512]{0,1:T(8,128)}, u32[]{:S(2)}) copy-start(f32[100,512]{0,1:T(8,128)} %copy-done.4) | copy-start | bytes 614404
  319.3 5.4 %copy-start.11 = (f32[4096]{0:T(1024)S(1)}, f32[4096]{0:T(1024)}, u32[]{:S(2)}) copy-start(f32[4096]{0:T(1024)} %param.16) | copy-start | bytes 49156
  319.3 6.0 %copy-start = (f32[100,4096]{0,1:T(8,128)S(1)}, f32[100,4096]{0,1:T(8,128)}, u32[]{:S(2)}) copy-start(f32[100,4096]{0,1:T(8,128)} %copy.33) | copy-start | bytes 4915204
Sparse Core Ops, SparseCore 0:
  92.5 20.9 all-reduce.3
  124.5 191.9 all-reduce.5
where the time goes:
time: 344 us; the launch traced here: 343 us
  waiting for transfers between devices  158 us (46%)
  local copies, waits for them, and re-layouts  82.2 us (24%)
  other arithmetic  51.8 us (15%)
  starting transfers between devices  22.4 us (7%)
  between operations  14.4 us (4%)
  matrix products  8.98 us (3%)
  blocking collectives  6 us (2%)
    psum x1, waiting for transfers between devices, per_device(): rel_total = lax.psum(local_rel, 'dom')  92 us
    ppermute x6, waiting for transfers between devices, from_behind(): return lax.ppermute(block, axis, route)  57.5 us
    gather x8, local copies, waits for them, and re-layouts, per_device(): negatives = jnp.where(chosen, block[:, neg_rows], negatives)  42.4 us
    scatter-add x4, other arithmetic, column_sum(): return empty.at[:, indices.reshape(-1)].add(values.reshape(full, -1))  22.7 us
    ppermute x6, starting transfers between devices, from_behind(): return lax.ppermute(block, axis, route)  22.1 us
    unnamed x46, local copies, waits for them, and re-layouts  19.2 us
    psum x1, waiting for transfers between devices, per_device(): pos, neg = lax.psum((pos_part, neg_part), 'dim')  8.05 us
  transfers between devices with their start and end apart: 8, of which 6 were waited for; matrix products, arithmetic and copies ran while one was open for 27% of the time, Pallas kernels for 0%

commit v1 on v0

v1 whole, which is shorter than its diff:
```python
import functools
import jax
import jax.numpy as jnp
from jax import lax
from jax.experimental import pallas as pl
from jax.experimental.pallas import tpu as pltpu
from jax.sharding import PartitionSpec as P

D = 400
STEPS = 4
RATE = 0.1
MESH = pl.DeviceIdType.MESH
HP = lax.Precision.HIGHEST
F32 = jnp.float32
BF16 = jnp.bfloat16
META = 16
LANES = 128


def split(x, n):
    parts = []
    for _ in range(n):
        part = x.astype(BF16)
        parts.append(part)
        x = x - part.astype(F32)
    return parts


def one_hot(row, first, count):
    rows = lax.broadcasted_iota(jnp.int32, (count, row.shape[1]), 0) + first
    return jnp.where(rows == row, 1.0, 0.0).astype(BF16)


def pick(x, hot, n):
    total = None
    for part in split(x, n):
        term = jnp.dot(part, hot, preferred_element_type=F32)
        total = term if total is None else total + term
    return total


def put(x, hot, n):
    total = None
    for part in split(x, n):
        term = lax.dot_general(part, hot, (((1,), (1,)), ((), ())), preferred_element_type=F32)
        total = term if total is None else total + term
    return total


def when(pred, fn):
    if isinstance(pred, bool):
        if pred:
            fn()
    else:
        pl.when(pred)(fn)


def wait_for(ref, sem):
    pltpu.make_async_copy(ref, ref, sem).wait()


def remote(src, dst, send, recv, device):
    return pltpu.make_async_remote_copy(
        src_ref=src, dst_ref=dst, send_sem=send, recv_sem=recv, device_id=device, device_id_type=MESH
    )


def query_kernel(
    n_dom, n_dim,
    ent_re, ent_im, rel_re, rel_im, lhs_ref, rhs_ref, ids_ref, neg_ref, bs_ref,
    grel, gent,
    qs, qr, mt, mr, bf, gqo, gqr, gbo, gbr, hs, rs,
    q_send, q_recv, m_send, m_recv, b_send, b_recv, g_send, g_recv, e_send, e_recv,
):
    p, d = lax.axis_index("dom"), lax.axis_index("dim")
    width, rows = ent_re.shape
    groups, per_edge = lhs_ref.shape
    rel_count = rel_re.shape[1]
    wp = qs.shape[1] // 2
    kp = 2 * wp
    units = groups * STEPS // n_dim

    def unit(td, i):
        if n_dim == groups:
            return i, td
        number = td + n_dim * i
        return lax.div(number, groups), lax.rem(number, groups)

    def holder(offset):
        return lax.rem(p + offset + n_dom, n_dom)

    def other(o):
        return lax.rem(d + o, n_dim)

    barrier = pltpu.get_barrier_semaphore()
    peers = 0
    for offset in range(1 - STEPS, STEPS):
        for o in range(n_dim):
            if offset != 0 or o != 0:
                pl.semaphore_signal(barrier, inc=1, device_id=(holder(offset), other(o)), device_id_type=MESH)
                peers += 1

    mt[...] = jnp.full(mt.shape, -1, jnp.int32)
    n_neg = neg_ref.shape[1]
    for g in range(groups):
        for j in range(0, n_neg, LANES):
            wide = min(LANES, n_neg - j)
            mt[g, j // LANES : j // LANES + 1, 0:wide] = neg_ref[g : g + 1, j : j + wide]
        mt[g, 8:9, :] = rhs_ref[g : g + 1, :]
        mt[g, 9:10, :] = jnp.broadcast_to(bs_ref[:, g : g + 1], (1, LANES))
    bf[d] = jnp.zeros((kp, rows), F32)
    bf[d, 0:width, :] = ent_re[...]
    bf[d, wp : wp + width, :] = ent_im[...]

    pl.semaphore_wait(barrier, peers)

    for o in range(1, n_dim):
        remote(bf.at[d], bf.at[d], b_send.at[o], b_recv.at[d], (p, other(o))).start()
    for i in range(units):
        s, g = unit(d, i)

        def local_meta(g=g, i=i):
            mr[i] = mt[g]

        def far_meta(s=s, g=g, i=i):
            remote(mt.at[g], mr.at[i], m_send.at[i], m_recv.at[i], (holder(-s), d)).start()

        when(s == 0, local_meta)
        when(s != 0, far_meta)

    lhs = jnp.concatenate([lhs_ref[g : g + 1, :] for g in range(groups)], 1)
    ids = jnp.concatenate([ids_ref[g : g + 1, :] for g in range(groups)], 1)
    hot_lhs = one_hot(lhs, 0, rows)
    h_re, h_im = pick(ent_re[...], hot_lhs, 3), pick(ent_im[...], hot_lhs, 3)
    chunk = 512

    def gather(c, carry):
        first = pl.multiple_of(c * chunk, chunk)
        hot = one_hot(ids, first, chunk)
        return (
            carry[0] + pick(rel_re[:, pl.ds(first, chunk)], hot, 3),
            carry[1] + pick(rel_im[:, pl.ds(first, chunk)], hot, 3),
        )

    empty = jnp.zeros((width, groups * per_edge), F32)
    r_re, r_im = lax.fori_loop(0, rel_count // chunk, gather, (empty, empty))
    hs[0:width, :] = h_re
    hs[wp : wp + width, :] = h_im
    rs[0:width, :] = r_re
    rs[wp : wp + width, :] = r_im
    q_re = h_re * r_re - h_im * r_im
    q_im = h_re * r_im + h_im * r_re
    qs[...] = jnp.zeros(qs.shape, F32)
    for g in range(groups):
        part = slice(g * per_edge, (g + 1) * per_edge)
        qs[g, 0:width, :] = q_re[:, part]
        qs[g, wp : wp + width, :] = q_im[:, part]

    for i in range(units):
        for o in range(n_dim):
            td = other(o)
            s, g = unit(td, i)

            def near_query(g=g, i=i):
                qr[i, d] = qs[g]

            def far_query(s=s, g=g, i=i, o=o, td=td):
                remote(qs.at[g], qr.at[i, d], q_send.at[i, o], q_recv.at[i, d], (holder(-s), td)).start()

            if o == 0:
                when(s == 0, near_query)
                when(s != 0, far_query)
            else:
                far_query()

    for o in range(1, n_dim):
        wait_for(bf.at[other(o)], b_recv.at[other(o)])

    at = lax.broadcasted_iota(jnp.int32, (rows, per_edge), 0)
    ones = jnp.ones((LANES, per_edge), BF16)
    for i in range(units):
        s, g = unit(d, i)
        when(s != 0, lambda i=i: wait_for(mr.at[i], m_recv.at[i]))
        hits = jnp.zeros((rows, LANES), F32)
        for j in range(8):
            hits = hits + jnp.where(at == mr[i, j : j + 1, :], 1.0, 0.0)
        cnt = jnp.dot(hits.astype(BF16), ones, preferred_element_type=F32)
        hit = at == mr[i, 8:9, :]
        live = jnp.where(mr[i, 9:10, :] == s, 1.0, 0.0)
        for o in range(n_dim):
            if o == 0:
                when(s != 0, lambda i=i: wait_for(qr.at[i, d], q_recv.at[i, d]))
            else:
                wait_for(qr.at[i, other(o)], q_recv.at[i, other(o)])
        block = bf[...].reshape(n_dim * kp, rows)
        q = qr[i].reshape(n_dim * kp, per_edge)
        st = lax.dot_general(block, q, (((0,), (0,)), ((), ())), precision=HP, preferred_element_type=F32)
        pos = jnp.sum(jnp.where(hit, st, 0.0), 0, keepdims=True)
        masked = jnp.where(cnt > 0.0, st, -3.0e38)
        top = jnp.maximum(jnp.max(masked, 0, keepdims=True), pos)
        e_neg = cnt * jnp.exp(masked - top)
        e_pos = jnp.exp(pos - top)
        scale = live / (e_pos + jnp.sum(e_neg, 0, keepdims=True))
        w = e_neg * scale + jnp.where(hit, e_pos * scale - live, 0.0)
        gq = jnp.dot(block, w, precision=HP, preferred_element_type=F32)
        gqo[i] = gq.reshape(n_dim, kp, per_edge)
        for o in range(n_dim):
            td = other(o)

            def near_grad(s=s, g=g, i=i):
                gqr[s, g] = gqo[i, d]

            def far_grad(s=s, g=g, i=i, o=o, td=td):
                remote(gqo.at[i, td], gqr.at[s, g], g_send.at[i, o], g_recv.at[s, g], (holder(s), td)).start()

            if o == 0:
                when(s == 0, near_grad)
                when(s != 0, far_grad)
            else:
                far_grad()
        gb = lax.dot_general(q, w, (((1,), (1,)), ((), ())), precision=HP, preferred_element_type=F32)
        gb = gb.reshape(n_dim, kp, rows)
        gbo[...] = gb if i == 0 else gbo[...] + gb
    for o in range(1, n_dim):
        remote(gbo.at[other(o)], gbr.at[d], e_send.at[o], e_recv.at[d], (p, other(o))).start()

    cols = []
    for g in range(groups):
        total = None
        for s in range(STEPS):
            handler = (s * groups + g) % n_dim
            if s == 0:
                when(d != handler, lambda s=s, g=g: wait_for(gqr.at[s, g], g_recv.at[s, g]))
            else:
                wait_for(gqr.at[s, g], g_recv.at[s, g])
            total = gqr[s, g] if total is None else total + gqr[s, g]
        cols.append(total)
    gq = jnp.concatenate(cols, 1)
    gq_re, gq_im = gq[0:width], gq[wp : wp + width]
    h_re, h_im = hs[0:width, :], hs[wp : wp + width, :]
    r_re, r_im = rs[0:width, :], rs[wp : wp + width, :]
    grel[...] = jnp.zeros(grel.shape, F32)
    grel[0:width, :] = gq_re * h_re + gq_im * h_im
    grel[wp : wp + width, :] = gq_im * h_re - gq_re * h_im
    grel[width : width + 1, :] = ids.astype(F32)
    gent[...] = gbo[d]
    for o in range(1, n_dim):
        wait_for(gbr.at[other(o)], e_recv.at[other(o)])
        gent[...] += gbr[other(o)]
    hot_lhs = one_hot(lhs, 0, rows)
    gent[0:width, :] += put(gq_re * r_re + gq_im * r_im, hot_lhs, 2)
    gent[wp : wp + width, :] += put(gq_im * r_re - gq_re * r_im, hot_lhs, 2)

    for o in range(1, n_dim):
        wait_for(bf.at[d], b_send.at[o])
        wait_for(gbo.at[d], e_send.at[o])
    for i in range(units):
        s, g = unit(d, i)
        when(s != 0, lambda i=i: wait_for(mt.at[0], m_send.at[i]))
        when(s != 0, lambda i=i: wait_for(qs.at[0], q_send.at[i, 0]))
        when(s != 0, lambda i=i: wait_for(gqo.at[i, 0], g_send.at[i, 0]))
        for o in range(1, n_dim):
            wait_for(qs.at[0], q_send.at[i, o])
            wait_for(gqo.at[i, 0], g_send.at[i, o])


def relation_kernel(
    n_dom, n_dim,
    grel, gent, ent_re, ent_im, ent_acc, rel_re, rel_im, rel_acc,
    new_re, new_im, new_acc, new_rre, new_rim, new_racc,
    slots, acc, esq, rsq,
    send, recv, eq_send, eq_recv, rq_send, rq_recv,
):
    p, d = lax.axis_index("dom"), lax.axis_index("dim")
    width = ent_re.shape[0]
    wp = grel.shape[0] // 2
    edges = grel.shape[1]
    rel_count = rel_re.shape[1]
    deep = n_dom // 4
    z, y, x = lax.div(p, 4), lax.rem(lax.div(p, 2), 2), lax.rem(p, 2)

    def index(zz, yy, xx):
        return zz * 4 + yy * 2 + xx

    def other(o):
        return lax.rem(d + o, n_dim)

    to_x, to_y = index(z, y, 1 - x), index(z, 1 - y, x)
    up, down = p + 4, p - 4
    has_up, has_down = z < deep - 1, z > 0

    barrier = pltpu.get_barrier_semaphore()
    for o in range(1, n_dim):
        pl.semaphore_signal(barrier, inc=1, device_id=(p, other(o)), device_id_type=MESH)
    for q in (to_x, to_y):
        pl.semaphore_signal(barrier, inc=1, device_id=(q, d), device_id_type=MESH)

    @pl.when(has_up)
    def _():
        pl.semaphore_signal(barrier, inc=1, device_id=(up, d), device_id_type=MESH)

    @pl.when(has_down)
    def _():
        pl.semaphore_signal(barrier, inc=1, device_id=(down, d), device_id_type=MESH)

    slots[p, 0] = grel[0:wp, :]
    slots[p, 1] = grel[wp : 2 * wp, :]
    pl.semaphore_wait(barrier, 1 + n_dim + jnp.minimum(z, 1) + jnp.minimum(deep - 1 - z, 1))

    def pass_on(j, half, way, target):
        remote(slots.at[j, half], slots.at[j, half], send.at[j, half, way], recv.at[j, half], (target, d)).start()

    def arrived(j, half):
        wait_for(slots.at[j, half], recv.at[j, half])

    def sent(j, half, way):
        wait_for(slots.at[j, half], send.at[j, half, way])

    def spread(j):
        pass_on(j, 0, 2, to_x)
        pass_on(j, 1, 3, to_y)
        pass_on(j, 0, 3, to_y)
        pass_on(j, 1, 2, to_x)

    def go_up(j):
        @pl.when(has_up)
        def _():
            pass_on(j, 0, 0, up)
            pass_on(j, 1, 0, up)

    def go_down(j):
        @pl.when(has_down)
        def _():
            pass_on(j, 0, 1, down)
            pass_on(j, 1, 1, down)

    go_up(p)
    go_down(p)
    spread(p)

    g_re, g_im = gent[0:width, :], gent[wp : wp + width, :]
    esq[d] = jnp.sum(g_re * g_re, 0, keepdims=True) + jnp.sum(g_im * g_im, 0, keepdims=True)
    for o in range(1, n_dim):
        remote(esq.at[d], esq.at[d], eq_send.at[o], eq_recv.at[d], (p, other(o))).start()

    chunk = 512

    def add_up(j):
        ids = slots[j, 0, width : width + 1, :].astype(jnp.int32)
        parts = split(slots[j].reshape(2 * wp, edges), 2)

        def body(c, carry):
            first = pl.multiple_of(c * chunk, chunk)
            hot = one_hot(ids, first, chunk)
            total = acc[:, pl.ds(first, chunk)]
            for part in parts:
                total = total + lax.dot_general(part, hot, (((1,), (1,)), ((), ())), preferred_element_type=F32)
            acc[:, pl.ds(first, chunk)] = total
            return carry

        lax.fori_loop(0, rel_count // chunk, body, 0)

    acc[...] = jnp.zeros(acc.shape, F32)

    def cross(zz):
        from_x, from_y = index(zz, y, 1 - x), index(zz, 1 - y, x)
        arrived(from_x, 0)
        pass_on(from_x, 0, 3, to_y)
        arrived(from_y, 1)
        pass_on(from_y, 1, 2, to_x)

    def column(k, carry):
        below, above = z - k, z + k

        @pl.when(below >= 0)
        def _():
            j = index(below, y, x)
            arrived(j, 0)
            arrived(j, 1)
            go_up(j)
            spread(j)

        @pl.when(above < deep)
        def _():
            j = index(above, y, x)
            arrived(j, 0)
            arrived(j, 1)
            go_down(j)
            spread(j)

        @pl.when(below + 1 >= 0)
        def _():
            cross(below + 1)
            add_up(index(below + 1, y, x))

        @pl.when((above - 1 < deep) & (k > 1))
        def _():
            cross(above - 1)
            add_up(index(above - 1, y, x))

        return carry

    lax.fori_loop(1, deep, column, 0)
    for far in (z - (deep - 1), z + (deep - 1)):

        @pl.when((far >= 0) & (far < deep))
        def _(far=far):
            cross(far)
            add_up(index(far, y, x))

    total = esq[d]
    for o in range(1, n_dim):
        wait_for(esq.at[other(o)], eq_recv.at[other(o)])
        total = total + esq[other(o)]
    total = ent_acc[...] + total / D
    new_acc[...] = total
    scale = RATE / jnp.sqrt(total)
    new_re[...] = ent_re[...] - scale * gent[0:width, :]
    new_im[...] = ent_im[...] - scale * gent[wp : wp + width, :]

    def rest(zz, carry):
        j = index(zz, y, 1 - x)
        arrived(j, 1)
        add_up(j)
        j = index(zz, 1 - y, x)
        arrived(j, 0)
        add_up(j)
        j = index(zz, 1 - y, 1 - x)
        arrived(j, 0)
        arrived(j, 1)
        add_up(j)
        return carry

    lax.fori_loop(0, deep, rest, 0)

    t_re, t_im = acc[0:width, :], acc[wp : wp + width, :]
    rsq[d] = jnp.sum(t_re * t_re, 0, keepdims=True) + jnp.sum(t_im * t_im, 0, keepdims=True)
    for o in range(1, n_dim):
        remote(rsq.at[d], rsq.at[d], rq_send.at[o], rq_recv.at[d], (p, other(o))).start()
    total = rsq[d]
    for o in range(1, n_dim):
        wait_for(rsq.at[other(o)], rq_recv.at[other(o)])
        total = total + rsq[other(o)]
    total = rel_acc[...] + total / D
    new_racc[...] = total
    scale = RATE / jnp.sqrt(total)
    new_rre[...] = rel_re[...] - scale * acc[0:width, :]
    new_rim[...] = rel_im[...] - scale * acc[wp : wp + width, :]

    def drain(zz, carry):
        j = index(zz, y, x)
        for half in (0, 1):

            @pl.when((zz <= z) & has_up)
            def _(half=half):
                sent(j, half, 0)

            @pl.when((zz >= z) & has_down)
            def _(half=half):
                sent(j, half, 1)

            sent(j, half, 2)
            sent(j, half, 3)
        sent(index(zz, y, 1 - x), 0, 3)
        sent(index(zz, 1 - y, x), 1, 2)
        return carry

    lax.fori_loop(0, deep, drain, 0)
    for o in range(1, n_dim):
        wait_for(esq.at[d], eq_send.at[o])
        wait_for(rsq.at[d], rq_send.at[o])


def per_device(
    n_dom, n_dim,
    ent_re, ent_im, ent_acc, rel_re, rel_im, rel_acc, lhs_rows, rhs_rows, rel_ids, neg_rows, bucket_step,
):
    width, rows = ent_re.shape
    rel_count = rel_re.shape[1]
    groups, per_edge = lhs_rows.shape
    wp = (width // 8 + 1) * 8
    kp = 2 * wp
    units = groups * STEPS // n_dim
    edges = groups * per_edge
    vmem = pl.BlockSpec(memory_space=pltpu.VMEM)
    dma = pltpu.SemaphoreType.DMA
    shape = jax.ShapeDtypeStruct
    grel, gent = pl.pallas_call(
        functools.partial(query_kernel, n_dom, n_dim),
        out_shape=(shape((kp, edges), F32), shape((kp, rows), F32)),
        in_specs=[vmem] * 9,
        out_specs=(vmem, vmem),
        scratch_shapes=[
            pltpu.VMEM((groups, kp, per_edge), F32),
            pltpu.VMEM((units, n_dim, kp, per_edge), F32),
            pltpu.VMEM((groups, META, LANES), jnp.int32),
            pltpu.VMEM((units, META, LANES), jnp.int32),
            pltpu.VMEM((n_dim, kp, rows), F32),
            pltpu.VMEM((units, n_dim, kp, per_edge), F32),
            pltpu.VMEM((STEPS, groups, kp, per_edge), F32),
            pltpu.VMEM((n_dim, kp, rows), F32),
            pltpu.VMEM((n_dim, kp, rows), F32),
            pltpu.VMEM((kp, edges), F32),
            pltpu.VMEM((kp, edges), F32),
            dma((units, n_dim)), dma((units, n_dim)),
            dma((units,)), dma((units,)),
            dma((n_dim,)), dma((n_dim,)),
            dma((units, n_dim)), dma((STEPS, groups)),
            dma((n_dim,)), dma((n_dim,)),
        ],
        compiler_params=pltpu.CompilerParams(
            collective_id=0, has_side_effects=True, vmem_limit_bytes=48 * 1024 * 1024
        ),
    )(ent_re, ent_im, rel_re, rel_im, lhs_rows, rhs_rows, rel_ids, neg_rows, bucket_step.reshape(1, groups))
    outs = pl.pallas_call(
        functools.partial(relation_kernel, n_dom, n_dim),
        out_shape=(
            shape((width, rows), F32), shape((width, rows), F32), shape((1, rows), F32),
            shape((width, rel_count), F32), shape((width, rel_count), F32), shape((1, rel_count), F32),
        ),
        in_specs=[vmem] * 8,
        out_specs=(vmem,) * 6,
        scratch_shapes=[
            pltpu.VMEM((n_dom, 2, wp, edges), F32),
            pltpu.VMEM((kp, rel_count), F32),
            pltpu.VMEM((n_dim, 1, rows), F32),
            pltpu.VMEM((n_dim, 1, rel_count), F32),
            dma((n_dom, 2, 4)), dma((n_dom, 2)),
            dma((n_dim,)), dma((n_dim,)),
            dma((n_dim,)), dma((n_dim,)),
        ],
        compiler_params=pltpu.CompilerParams(
            collective_id=1, has_side_effects=True, vmem_limit_bytes=48 * 1024 * 1024
        ),
    )(
        grel, gent, ent_re, ent_im, ent_acc.reshape(1, rows), rel_re, rel_im, rel_acc.reshape(1, rel_count)
    )
    return outs[0], outs[1], outs[2].reshape(rows), outs[3], outs[4], outs[5].reshape(rel_count)


def solution(mesh):
    return jax.shard_map(
        functools.partial(per_device, mesh.shape["dom"], mesh.shape["dim"]),
        mesh=mesh,
        in_specs=(
            P("dim", "dom"),
            P("dim", "dom"),
            P("dom"),
            P("dim", None),
            P("dim", None),
            P(),
            P("dom", None),
            P("dom", None),
            P("dom", None),
            P("dom", None),
            P("dom"),
        ),
        out_specs=(P("dim", "dom"), P("dim", "dom"), P("dom"), P("dim", None), P("dim", None), P()),
        check_vma=False,
    )
```

time: 344 us -> 127 us (0.37)
  waiting for transfers between devices: 158 us -> 0 us
  Pallas kernels: 0 us -> 113 us
  local copies, waits for them, and re-layouts: 82.2 us -> 13.1 us
  other arithmetic: 51.8 us -> 0 us
  starting transfers between devices: 22.4 us -> 0 us
  between operations: 14.4 us -> 0.69 us
  matrix products: 8.98 us -> 0 us
  blocking collectives: 6 us -> 0 us
    pallas_call x0 -> x2, Pallas kernels: none -> 113 us  [the longest x1 68.2 us: per_device(): pl.pallas_call(functools.partial(relation_kernel, n_dom, n_dim), out_shap...]
    psum x2 -> x0, waiting for transfers between devices: 100 us -> none  [the longest x1 92 us: per_device(): rel_total = lax.psum(local_rel, 'dom')]
    ppermute x6 -> x0, waiting for transfers between devices: 57.5 us -> none  [from_behind(): return lax.ppermute(block, axis, route)]
    gather x20 -> x0, local copies, waits for them, and re-layouts: 53.2 us -> none  [the longest x8 42.4 us: per_device(): negatives = jnp.where(chosen, block[:, neg_rows], negatives)]
    scatter-add x4 -> x0, other arithmetic: 22.7 us -> none  [column_sum(): return empty.at[:, indices.reshape(-1)].add(values.reshape(full, -1))]
    ppermute x6 -> x0, starting transfers between devices: 22.1 us -> none  [from_behind(): return lax.ppermute(block, axis, route)]
    dot_general x3 -> x0, matrix products: 8.98 us -> none  [the longest x1 4.39 us: per_device(): neg_part = jnp.einsum('kce,kcn->cen', query, negatives, precision=hp)]
    unnamed x46 -> x28, local copies, waits for them, and re-layouts: 19.2 us -> 13.1 us
  transfers between devices with their start and end apart: 8 -> 0, of which waited for: 6 -> 0; matrix products, arithmetic and copies ran while one was open for 27% -> 0% of each run, Pallas kernels for 0% -> 0%
where the time goes in v1:
time: 127 us; the launch traced here: 126 us
  Pallas kernels  113 us (89%)
  local copies, waits for them, and re-layouts  13.1 us (10%)
    pallas_call x1, Pallas kernels, per_device(): pl.pallas_call(functools.partial(relation_kernel, n_dom, n_dim), out_shap...  68.2 us
    pallas_call x1, Pallas kernels, per_device(): pl.pallas_call(functools.partial(query_kernel, n_dom, n_dim), out_shape=(...  44.5 us
    unnamed x28, local copies, waits for them, and re-layouts  13.1 us

profile of v1, /device:TPU:0, one launch (start us, length us, event | category | flops | bytes accessed | tf_op | source)
XLA Modules:
  0.0 126.5 jit_solution(11875334850176416744)
XLA Ops:
  0.6 0.0 copy-start
  0.6 1.4 %copy-done = f32[100,4096]{1,0:T(8,128)S(1)} copy-done((f32[100,4096]{1,0:T(8,128)S(1)}, f32[100,4096]{1,0:T(8,128)}, u32[]{:S(2)}) %copy-start) | copy-done | bytes 1638424
  2.1 0.0 copy-start.1
  2.1 1.5 %copy-done.1 = f32[100,4096]{1,0:T(8,128)S(1)} copy-done((f32[100,4096]{1,0:T(8,128)S(1)}, f32[100,4096]{1,0:T(8,128)}, u32[]{:S(2)}) %copy-start.1) | copy-done | bytes 1638424
  3.5 0.0 copy-start.2
  3.5 0.9 copy-done.2
  4.5 0.0 copy-start.3
  4.5 0.9 copy-done.3
  5.4 0.0 copy-start.5
  5.4 0.7 copy-done.5
  6.1 0.0 copy-start.7
  6.1 0.7 copy-done.7
  6.8 0.0 copy-start.8
  6.8 0.7 copy-done.8
  7.5 0.0 copy-start.9
  7.5 0.7 copy-done.9
  8.1 0.0 copy-start.10
  8.2 0.7 copy-done.10
  8.8 0.0 copy-start.4
  8.8 0.0 copy-start.6
  8.8 44.5 %shard_map.154 = (f32[208,256]{1,0:T(8,128)S(1)}, f32[208,512]{1,0:T(8,128)S(1)}) custom-call(f32[100,512]{1,0:T(8,128)S(1)} %copy-done.2, f32[100,512]{1,0:T(8,128)S(1)} %copy-done.3, f32[100,4096]{1,0:T(8,128)S(1)} %copy-done, f32[100,4096]{1,0:T(8,128)S(1)} %copy-done.1, s32[2,128]{1,0:T(2,128)S(1)} %copy-done.7, s32[2,128]{1,0:T(2,128)S(1)} %copy-done.8, ...), custom_call_target="tpu_custom_call" | custom-call | tf_op jit(solution)/shard_map/pallas_call | solution.py:488
  53.3 0.0 copy-done.4
  53.3 0.0 copy-done.6
  53.3 68.2 %shard_map.155 = (f32[100,512]{1,0:T(8,128)S(1)}, f32[100,512]{1,0:T(8,128)S(1)}, f32[1,512]{1,0:T(1,128)S(1)}, f32[100,4096]{1,0:T(8,128)S(1)}, f32[100,4096]{1,0:T(8,128)S(1)}, /*index=5*/f32[1,4096]{1,0:T(1,128)S(1)}) custom-call(f32[208,256]{1,0:T(8,128)S(1)} %get-tuple-element.14.grel, f32[208,512]{1,0:T(8,128)S(1)} %get-tuple-element.15.gent, ...), custom_call_target="tpu_custom_call" | custom-call | tf_op jit(solution)/shard_map/pallas_call | solution.py:515
  121.6 0.7 copy.23
  122.2 0.7 copy.24
  122.9 0.6 copy.25
  123.5 1.2 copy.26
  124.7 1.2 copy.27
  125.9 0.6 copy.28
Async XLA Ops:
  0.6 1.5 %copy-start = (f32[100,4096]{1,0:T(8,128)S(1)}, f32[100,4096]{1,0:T(8,128)}, u32[]{:S(2)}) copy-start(f32[100,4096]{1,0:T(8,128)} %rel_re.3) | copy-start | bytes 4915204
  2.1 1.5 %copy-start.1 = (f32[100,4096]{1,0:T(8,128)S(1)}, f32[100,4096]{1,0:T(8,128)}, u32[]{:S(2)}) copy-start(f32[100,4096]{1,0:T(8,128)} %rel_im.3) | copy-start | bytes 4915204
  3.5 0.9 copy-start.2
  4.5 0.9 copy-start.3
  5.4 0.7 copy-start.5
  6.1 0.7 copy-start.7
  6.8 0.7 copy-start.8
  7.5 0.7 copy-start.9
  8.1 0.7 copy-start.10
  8.8 44.5 %copy-start.4 = (f32[4096]{0:T(1024)S(1)}, f32[4096]{0:T(1024)}, u32[]{:S(2)}) copy-start(f32[4096]{0:T(1024)} %param.16) | copy-start | bytes 49156
  8.8 44.5 %copy-start.6 = (f32[512]{0:T(512)S(1)}, f32[512]{0:T(512)}, u32[]{:S(2)}) copy-start(f32[512]{0:T(512)} %param.13) | copy-start | bytes 6148

commit v2 on v1

v2 whole, which is shorter than its diff:
```python
import functools
import jax
import jax.numpy as jnp
from jax import lax
from jax.experimental import pallas as pl
from jax.experimental.pallas import tpu as pltpu
from jax.sharding import PartitionSpec as P

D = 400
STEPS = 4
RATE = 0.1
MESH = pl.DeviceIdType.MESH
F32 = jnp.float32
BF16 = jnp.bfloat16
META = 16
LANES = 128


def split(x, n):
    parts = []
    for _ in range(n):
        part = x.astype(BF16)
        parts.append(part)
        x = x - part.astype(F32)
    return parts


def one_hot(row, first, count):
    rows = lax.broadcasted_iota(jnp.int32, (count, row.shape[1]), 0) + first
    return jnp.where(rows == row, 1.0, 0.0).astype(BF16)


def pick(x, hot, n):
    total = None
    for part in split(x, n):
        term = jnp.dot(part, hot, preferred_element_type=F32)
        total = term if total is None else total + term
    return total


def put(x, hot, n):
    total = None
    for part in split(x, n):
        term = lax.dot_general(part, hot, (((1,), (1,)), ((), ())), preferred_element_type=F32)
        total = term if total is None else total + term
    return total


def when(pred, fn):
    if isinstance(pred, bool):
        if pred:
            fn()
    else:
        pl.when(pred)(fn)


def wait_for(ref, sem):
    pltpu.make_async_copy(ref, ref, sem).wait()


def remote(src, dst, send, recv, device):
    return pltpu.make_async_remote_copy(
        src_ref=src, dst_ref=dst, send_sem=send, recv_sem=recv, device_id=device, device_id_type=MESH
    )


def round_kernel(
    n_dom, n_dim,
    ent_re_in, ent_im_in, ent_acc_in, rel_re_in, rel_im_in, rel_acc_in, lhs_in, rhs_in, ids_in, neg_in, bs_in,
    new_re, new_im, new_acc, new_rre, new_rim, new_racc,
    ent_re, ent_im, ent_acc, rel_re, rel_im, rel_acc, lhs_ref, rhs_ref, ids_ref, neg_ref, bs_ref,
    qs, qr, mt, mr, bf, bt, bp, wts, gqo, gqr, gbo, gbr, gent,
    slots, acc, batch, esq, rsq,
    in_sem,
    q_send, q_recv, m_send, m_recv, b_send, b_recv, g_send, g_recv, e_send, e_recv,
    send, recv, eq_send, eq_recv, rq_send, rq_recv,
):
    p, d = lax.axis_index("dom"), lax.axis_index("dim")
    width, rows = ent_re.shape
    groups, per_edge = lhs_ref.shape
    edges = groups * per_edge
    rel_count = rel_re.shape[1]
    kp = qs.shape[1]
    wp = kp // 2
    units = groups * STEPS // n_dim
    deep = n_dom // 4
    z, y, x = lax.div(p, 4), lax.rem(lax.div(p, 2), 2), lax.rem(p, 2)

    def index(zz, yy, xx):
        return zz * 4 + yy * 2 + xx

    def unit(td, i):
        if n_dim == groups:
            return i, td
        number = td + n_dim * i
        return lax.div(number, groups), lax.rem(number, groups)

    def holder(offset):
        return lax.rem(p + offset + n_dom, n_dom)

    def other(o):
        return lax.rem(d + o, n_dim)

    to_x, to_y = index(z, y, 1 - x), index(z, 1 - y, x)
    up, down = p + 4, p - 4
    has_up, has_down = z < deep - 1, z > 0

    barrier = pltpu.get_barrier_semaphore()

    def greet(dom, dim):
        pl.semaphore_signal(barrier, inc=1, device_id=(dom, dim), device_id_type=MESH)

    peers = 0
    for offset in range(1 - STEPS, STEPS):
        for o in range(n_dim):
            if offset != 0 or o != 0:
                greet(holder(offset), other(o))
                peers += 1
    greet(to_x, d)
    greet(to_y, d)

    @pl.when(has_up)
    def _():
        greet(up, d)

    @pl.when(has_down)
    def _():
        greet(down, d)

    fetches = []
    for k, (src, dst) in enumerate([
        (lhs_in, lhs_ref), (rhs_in, rhs_ref), (ids_in, ids_ref), (neg_in, neg_ref), (bs_in, bs_ref),
        (ent_re_in, ent_re), (ent_im_in, ent_im), (rel_re_in, rel_re), (rel_im_in, rel_im),
        (ent_acc_in, ent_acc), (rel_acc_in, rel_acc),
    ]):
        fetches.append(pltpu.make_async_copy(src, dst, in_sem.at[k]))
        fetches[-1].start()
    mt[...] = jnp.full(mt.shape, -1, jnp.int32)
    qs[...] = jnp.zeros(qs.shape, F32)
    for half in (0, 1):
        slots[p, half] = jnp.zeros((wp, edges), F32)
    bf[d] = jnp.zeros((kp, rows), F32)
    for fetch in fetches[:7]:
        fetch.wait()

    n_neg = neg_ref.shape[1]
    for g in range(groups):
        for j in range(0, n_neg, LANES):
            wide = min(LANES, n_neg - j)
            mt[g, j // LANES : j // LANES + 1, 0:wide] = neg_ref[g : g + 1, j : j + wide]
        mt[g, 8:9, :] = rhs_ref[g : g + 1, :]
        mt[g, 9:10, :] = jnp.broadcast_to(bs_ref[:, g : g + 1], (1, LANES))
    bf[d, 0:width, :] = ent_re[...]
    bf[d, wp : wp + width, :] = ent_im[...]

    pl.semaphore_wait(barrier, peers + 2 + jnp.minimum(z, 1) + jnp.minimum(deep - 1 - z, 1))

    for i in range(units):
        s, g = unit(d, i)

        def local_meta(g=g, i=i):
            mr[i] = mt[g]

        def far_meta(s=s, g=g, i=i):
            remote(mt.at[g], mr.at[i], m_send.at[i], m_recv.at[i], (holder(-s), d)).start()

        when(s == 0, local_meta)
        when(s != 0, far_meta)
    for o in range(1, n_dim):
        remote(bf.at[d], bf.at[d], b_send.at[o], b_recv.at[d], (p, other(o))).start()

    lhs = jnp.concatenate([lhs_ref[g : g + 1, :] for g in range(groups)], 1)
    ids = jnp.concatenate([ids_ref[g : g + 1, :] for g in range(groups)], 1)
    hot_lhs = one_hot(lhs, 0, rows)
    h_re, h_im = pick(ent_re[...], hot_lhs, 3), pick(ent_im[...], hot_lhs, 3)
    for fetch in fetches[7:]:
        fetch.wait()
    chunk = 512

    def gather(c, carry):
        first = pl.multiple_of(c * chunk, chunk)
        hot = one_hot(ids, first, chunk)
        return (
            carry[0] + pick(rel_re[:, pl.ds(first, chunk)], hot, 3),
            carry[1] + pick(rel_im[:, pl.ds(first, chunk)], hot, 3),
        )

    empty = jnp.zeros((width, edges), F32)
    r_re, r_im = lax.fori_loop(0, rel_count // chunk, gather, (empty, empty))
    q_re = h_re * r_re - h_im * r_im
    q_im = h_re * r_im + h_im * r_re
    for g in range(groups):
        part = slice(g * per_edge, (g + 1) * per_edge)
        qs[g, 0:width, :] = q_re[:, part]
        qs[g, wp : wp + width, :] = q_im[:, part]

    for i in reversed(range(units)):
        for o in range(n_dim):
            td = other(o)
            s, g = unit(td, i)

            def near_query(g=g, i=i):
                qr[i, d] = qs[g]

            def far_query(s=s, g=g, i=i, o=o, td=td):
                remote(qs.at[g], qr.at[i, d], q_send.at[i, o], q_recv.at[i, d], (holder(-s), td)).start()

            if o == 0:
                when(s == 0, near_query)
                when(s != 0, far_query)
            else:
                far_query()

    for o in range(1, n_dim):
        wait_for(bf.at[other(o)], b_recv.at[other(o)])
    deep_k = n_dim * kp
    block = bf[...].reshape(deep_k, rows)
    for k, part in enumerate(split(block, 2)):
        bp[k] = part
    for k, part in enumerate(split(jnp.transpose(block), 3)):
        bt[k] = part

    at = lax.broadcasted_iota(jnp.int32, (rows, per_edge), 0)
    ones = jnp.ones((LANES, per_edge), BF16)

    def dot(a, b):
        return jnp.dot(a, b, preferred_element_type=F32)

    for i in range(units):
        s, g = unit(d, i)
        when(s != 0, lambda i=i: wait_for(mr.at[i], m_recv.at[i]))
        hits = jnp.zeros((rows, LANES), F32)
        for j in range(8):
            hits = hits + jnp.where(at == mr[i, j : j + 1, :], 1.0, 0.0)
        cnt = dot(hits.astype(BF16), ones)
        hit = at == mr[i, 8:9, :]
        live = jnp.where(mr[i, 9:10, :] == s, 1.0, 0.0)
        for o in range(n_dim):
            if o == 0:
                when(s != 0, lambda i=i: wait_for(qr.at[i, d], q_recv.at[i, d]))
            else:
                wait_for(qr.at[i, other(o)], q_recv.at[i, other(o)])
        q0, q1, q2 = split(qr[i].reshape(deep_k, per_edge), 3)
        b0, b1, b2 = bt[0], bt[1], bt[2]
        st = dot(b0, q0) + (dot(b0, q1) + dot(b1, q0)) + (dot(b0, q2) + dot(b2, q0) + dot(b1, q1))
        pos = jnp.sum(jnp.where(hit, st, 0.0), 0, keepdims=True)
        masked = jnp.where(cnt > 0.0, st, -3.0e38)
        top = jnp.maximum(jnp.max(masked, 0, keepdims=True), pos)
        e_neg = cnt * jnp.exp(masked - top)
        e_pos = jnp.exp(pos - top)
        scale = live / (e_pos + jnp.sum(e_neg, 0, keepdims=True))
        w = e_neg * scale + jnp.where(hit, e_pos * scale - live, 0.0)
        w0, w1 = split(w, 2)
        wts[0, :, i * per_edge : (i + 1) * per_edge] = w0
        wts[1, :, i * per_edge : (i + 1) * per_edge] = w1
        gq = dot(bp[0], w0) + (dot(bp[0], w1) + dot(bp[1], w0))
        gqo[i] = gq.reshape(n_dim, kp, per_edge)
        for o in range(n_dim):
            td = other(o)

            def near_grad(s=s, g=g, i=i):
                gqr[s, g] = gqo[i, d]

            def far_grad(s=s, g=g, i=i, o=o, td=td):
                remote(gqo.at[i, td], gqr.at[s, g], g_send.at[i, o], g_recv.at[s, g], (holder(s), td)).start()

            if o == 0:
                when(s == 0, near_grad)
                when(s != 0, far_grad)
            else:
                far_grad()
    q = jnp.concatenate([qr[i].reshape(deep_k, per_edge) for i in range(units)], 1)
    q0, q1 = split(q, 2)
    turned = (((1,), (1,)), ((), ()))
    gb = lax.dot_general(q0, wts[0], turned, preferred_element_type=F32)
    gb = gb + lax.dot_general(q0, wts[1], turned, preferred_element_type=F32)
    gb = gb + lax.dot_general(q1, wts[0], turned, preferred_element_type=F32)
    gbo[...] = gb.reshape(n_dim, kp, rows)
    for o in range(1, n_dim):
        remote(gbo.at[other(o)], gbr.at[d], e_send.at[o], e_recv.at[d], (p, other(o))).start()

    cols = []
    for g in range(groups):
        total = None
        for s in range(STEPS):
            handler = (s * groups + g) % n_dim
            if s == 0:
                when(d != handler, lambda s=s, g=g: wait_for(gqr.at[s, g], g_recv.at[s, g]))
            else:
                wait_for(gqr.at[s, g], g_recv.at[s, g])
            total = gqr[s, g] if total is None else total + gqr[s, g]
        cols.append(total)
    gq = jnp.concatenate(cols, 1)
    gq_re, gq_im = gq[0:width], gq[wp : wp + width]
    slots[p, 0, 0:width, :] = gq_re * h_re + gq_im * h_im
    slots[p, 1, 0:width, :] = gq_im * h_re - gq_re * h_im
    slots[p, 0, width : width + 1, :] = ids.astype(F32)

    def pass_on(j, half, way, target):
        remote(slots.at[j, half], slots.at[j, half], send.at[j, half, way], recv.at[j, half], (target, d)).start()

    def arrived(j, half):
        wait_for(slots.at[j, half], recv.at[j, half])

    def sent(j, half, way):
        wait_for(slots.at[j, half], send.at[j, half, way])

    def spread(j):
        pass_on(j, 0, 2, to_x)
        pass_on(j, 1, 3, to_y)
        pass_on(j, 0, 3, to_y)
        pass_on(j, 1, 2, to_x)

    def go_up(j):
        @pl.when(has_up)
        def _():
            pass_on(j, 0, 0, up)
            pass_on(j, 1, 0, up)

    def go_down(j):
        @pl.when(has_down)
        def _():
            pass_on(j, 0, 1, down)
            pass_on(j, 1, 1, down)

    go_up(p)
    go_down(p)
    spread(p)

    gent[...] = gbo[d]
    for o in range(1, n_dim):
        wait_for(gbr.at[other(o)], e_recv.at[other(o)])
        gent[...] += gbr[other(o)]
    gent[0:width, :] += put(gq_re * r_re + gq_im * r_im, hot_lhs, 2)
    gent[wp : wp + width, :] += put(gq_im * r_re - gq_re * r_im, hot_lhs, 2)
    g_re, g_im = gent[0:width, :], gent[wp : wp + width, :]
    esq[d] = jnp.sum(g_re * g_re, 0, keepdims=True) + jnp.sum(g_im * g_im, 0, keepdims=True)
    for o in range(1, n_dim):
        remote(esq.at[d], esq.at[d], eq_send.at[o], eq_recv.at[d], (p, other(o))).start()

    def cross(zz):
        from_x, from_y = index(zz, y, 1 - x), index(zz, 1 - y, x)
        arrived(from_x, 0)
        pass_on(from_x, 0, 3, to_y)
        arrived(from_y, 1)
        pass_on(from_y, 1, 2, to_x)

    def column(k, carry):
        below, above = z - k, z + k

        @pl.when(below >= 0)
        def _():
            j = index(below, y, x)
            arrived(j, 0)
            arrived(j, 1)
            go_up(j)
            spread(j)

        @pl.when(above < deep)
        def _():
            j = index(above, y, x)
            arrived(j, 0)
            arrived(j, 1)
            go_down(j)
            spread(j)

        @pl.when(below + 1 >= 0)
        def _():
            cross(below + 1)

        @pl.when((above - 1 < deep) & (k > 1))
        def _():
            cross(above - 1)

        return carry

    lax.fori_loop(1, deep, column, 0)
    for far in (z - (deep - 1), z + (deep - 1)):

        @pl.when((far >= 0) & (far < deep))
        def _(far=far):
            cross(far)

    per_batch = batch.shape[1] // edges
    piece = min(256, rel_count)
    labels = lax.broadcasted_iota(jnp.int32, (piece, per_batch * edges), 0).astype(F32).astype(BF16)

    def add_up(js, fresh):
        names = []
        for k, j in enumerate(js):
            cut = slice(k * edges, (k + 1) * edges)
            high, low = split(slots[j].reshape(kp, edges), 2)
            batch[0:kp, cut] = high
            batch[kp : 2 * kp, cut] = low
            names.append(slots[j, 0, width : width + 1, :])
        names = jnp.concatenate(names, 1)

        def body(c, carry):
            first = pl.multiple_of(c * piece, piece)
            mine = (names - first.astype(F32)).astype(BF16)
            hot = jnp.where(labels == mine, jnp.ones((), BF16), jnp.zeros((), BF16))
            both = lax.dot_general(batch[...], hot, turned, preferred_element_type=F32)
            total = both[0:kp] + both[kp : 2 * kp]
            if not fresh:
                total = total + acc[:, pl.ds(first, piece)]
            acc[:, pl.ds(first, piece)] = total
            return carry

        lax.fori_loop(0, rel_count // piece, body, 0)

    add_up([index(zz, y, x) for zz in range(per_batch)], True)
    for lot in range(1, deep // per_batch):
        add_up([index(lot * per_batch + zz, y, x) for zz in range(per_batch)], False)

    total = esq[d]
    for o in range(1, n_dim):
        wait_for(esq.at[other(o)], eq_recv.at[other(o)])
        total = total + esq[other(o)]
    total = ent_acc[...] + total / D
    new_acc[...] = total
    scale = RATE / jnp.sqrt(total)
    new_re[...] = ent_re[...] - scale * gent[0:width, :]
    new_im[...] = ent_im[...] - scale * gent[wp : wp + width, :]

    for yy, xx, halves in ((y, 1 - x, (1,)), (1 - y, x, (0,)), (1 - y, 1 - x, (0, 1))):

        def rest(lot, carry, yy=yy, xx=xx, halves=halves):
            js = [index(lot * per_batch + zz, yy, xx) for zz in range(per_batch)]
            for j in js:
                for half in halves:
                    arrived(j, half)
            add_up(js, False)
            return carry

        lax.fori_loop(0, deep // per_batch, rest, 0)

    t_re, t_im = acc[0:width, :], acc[wp : wp + width, :]
    rsq[d] = jnp.sum(t_re * t_re, 0, keepdims=True) + jnp.sum(t_im * t_im, 0, keepdims=True)
    for o in range(1, n_dim):
        remote(rsq.at[d], rsq.at[d], rq_send.at[o], rq_recv.at[d], (p, other(o))).start()
    total = rsq[d]
    for o in range(1, n_dim):
        wait_for(rsq.at[other(o)], rq_recv.at[other(o)])
        total = total + rsq[other(o)]
    total = rel_acc[...] + total / D
    new_racc[...] = total
    scale = RATE / jnp.sqrt(total)
    new_rre[...] = rel_re[...] - scale * acc[0:width, :]
    new_rim[...] = rel_im[...] - scale * acc[wp : wp + width, :]

    def drain(zz, carry):
        j = index(zz, y, x)
        for half in (0, 1):

            @pl.when((zz <= z) & has_up)
            def _(half=half):
                sent(j, half, 0)

            @pl.when((zz >= z) & has_down)
            def _(half=half):
                sent(j, half, 1)

            sent(j, half, 2)
            sent(j, half, 3)
        sent(index(zz, y, 1 - x), 0, 3)
        sent(index(zz, 1 - y, x), 1, 2)
        return carry

    lax.fori_loop(0, deep, drain, 0)
    for o in range(1, n_dim):
        wait_for(bf.at[d], b_send.at[o])
        wait_for(gbo.at[d], e_send.at[o])
        wait_for(esq.at[d], eq_send.at[o])
        wait_for(rsq.at[d], rq_send.at[o])
    for i in range(units):
        s, g = unit(d, i)
        when(s != 0, lambda i=i: wait_for(mt.at[0], m_send.at[i]))
        when(s != 0, lambda i=i: wait_for(qs.at[0], q_send.at[i, 0]))
        when(s != 0, lambda i=i: wait_for(gqo.at[i, 0], g_send.at[i, 0]))
        for o in range(1, n_dim):
            wait_for(qs.at[0], q_send.at[i, o])
            wait_for(gqo.at[i, 0], g_send.at[i, o])


def per_device(
    n_dom, n_dim,
    ent_re, ent_im, ent_acc, rel_re, rel_im, rel_acc, lhs_rows, rhs_rows, rel_ids, neg_rows, bucket_step,
):
    width, rows = ent_re.shape
    rel_count = rel_re.shape[1]
    groups, per_edge = lhs_rows.shape
    wp = (width // 8 + 1) * 8
    kp = 2 * wp
    units = groups * STEPS // n_dim
    edges = groups * per_edge
    deep_k = n_dim * kp
    vmem = pl.BlockSpec(memory_space=pltpu.VMEM)
    hbm = pl.BlockSpec(memory_space=pl.ANY)
    dma = pltpu.SemaphoreType.DMA
    shape = jax.ShapeDtypeStruct
    args = (
        ent_re, ent_im, ent_acc.reshape(1, rows), rel_re, rel_im, rel_acc.reshape(1, rel_count),
        lhs_rows, rhs_rows, rel_ids, neg_rows, bucket_step.reshape(1, groups),
    )
    outs = pl.pallas_call(
        functools.partial(round_kernel, n_dom, n_dim),
        out_shape=tuple(shape(a.shape, F32) for a in args[:6]),
        in_specs=[hbm] * len(args),
        out_specs=(vmem,) * 6,
        scratch_shapes=[pltpu.VMEM(a.shape, a.dtype) for a in args] + [
            pltpu.VMEM((groups, kp, per_edge), F32),
            pltpu.VMEM((units, n_dim, kp, per_edge), F32),
            pltpu.VMEM((groups, META, LANES), jnp.int32),
            pltpu.VMEM((units, META, LANES), jnp.int32),
            pltpu.VMEM((n_dim, kp, rows), F32),
            pltpu.VMEM((3, rows, deep_k), BF16),
            pltpu.VMEM((2, deep_k, rows), BF16),
            pltpu.VMEM((2, rows, units * per_edge), BF16),
            pltpu.VMEM((units, n_dim, kp, per_edge), F32),
            pltpu.VMEM((STEPS, groups, kp, per_edge), F32),
            pltpu.VMEM((n_dim, kp, rows), F32),
            pltpu.VMEM((n_dim, kp, rows), F32),
            pltpu.VMEM((kp, rows), F32),
            pltpu.VMEM((n_dom, 2, wp, edges), F32),
            pltpu.VMEM((kp, rel_count), F32),
            pltpu.VMEM((2 * kp, 4 * edges), BF16),
            pltpu.VMEM((n_dim, 1, rows), F32),
            pltpu.VMEM((n_dim, 1, rel_count), F32),
            dma((len(args),)),
            dma((units, n_dim)), dma((units, n_dim)),
            dma((units,)), dma((units,)),
            dma((n_dim,)), dma((n_dim,)),
            dma((units, n_dim)), dma((STEPS, groups)),
            dma((n_dim,)), dma((n_dim,)),
            dma((n_dom, 2, 4)), dma((n_dom, 2)),
            dma((n_dim,)), dma((n_dim,)),
            dma((n_dim,)), dma((n_dim,)),
        ],
        compiler_params=pltpu.CompilerParams(
            collective_id=0, has_side_effects=True, vmem_limit_bytes=60 * 1024 * 1024
        ),
    )(*args)
    return outs[0], outs[1], outs[2].reshape(rows), outs[3], outs[4], outs[5].reshape(rel_count)


def solution(mesh):
    return jax.shard_map(
        functools.partial(per_device, mesh.shape["dom"], mesh.shape["dim"]),
        mesh=mesh,
        in_specs=(
            P("dim", "dom"),
            P("dim", "dom"),
            P("dom"),
            P("dim", None),
            P("dim", None),
            P(),
            P("dom", None),
            P("dom", None),
            P("dom", None),
            P("dom", None),
            P("dom"),
        ),
        out_specs=(P("dim", "dom"), P("dim", "dom"), P("dom"), P("dim", None), P("dim", None), P()),
        check_vma=False,
    )
```

time: 127 us -> 117 us (0.921)
  Pallas kernels: 113 us -> 106 us
  local copies, waits for them, and re-layouts: 13.1 us -> 9.21 us
    pallas_call x2 -> x1, Pallas kernels: 113 us -> 106 us  [per_device(): pl.pallas_call(functools.partial(round_kernel, n_dom, n_dim), out_shape=t...]
    unnamed x28 -> x10, local copies, waits for them, and re-layouts: 13.1 us -> 9.21 us
where the time goes in v2:
time: 117 us; the launch traced here: 116 us
  Pallas kernels  106 us (91%)
  local copies, waits for them, and re-layouts  9.21 us (8%)
    pallas_call x1, Pallas kernels, per_device(): pl.pallas_call(functools.partial(round_kernel, n_dom, n_dim), out_shape=t...  106 us
    unnamed x10, local copies, waits for them, and re-layouts  9.21 us

profile of v2, /device:TPU:0, one launch (start us, length us, event | category | flops | bytes accessed | tf_op | source)
XLA Modules:
  0.0 116.1 jit_solution(13062214980220133369)
XLA Ops:
  0.6 106.3 %shard_map.154 = (f32[100,512]{1,0:T(8,128)}, f32[100,512]{1,0:T(8,128)}, f32[1,512]{1,0:T(1,128)}, f32[100,4096]{1,0:T(8,128)}, f32[100,4096]{1,0:T(8,128)}, /*index=5*/f32[1,4096]{1,0:T(1,128)}) custom-call(f32[100,512]{1,0:T(8,128)} %ent_re_in.1, f32[100,512]{1,0:T(8,128)} %ent_im_in.1, f32[1,512]{1,0:T(1,128)} %bitcast.7, f32[100,4096]{1,0:T(8,128)} %rel_re_in.1, ...), custom_call_target="tpu_custom_call" | custom-call | tf_op jit(solution)/shard_map/pallas_call | solution.py:505
  106.9 1.6 %copy.23 = f32[100,512]{1,0:T(8,128)} copy(f32[100,512]{1,0:T(8,128)} %get-tuple-element.24) | data formatting | bytes 409600
  108.5 1.6 %copy.24 = f32[100,512]{1,0:T(8,128)} copy(f32[100,512]{1,0:T(8,128)} %get-tuple-element.25) | data formatting | bytes 409600
  110.2 1.3 %copy.25 = f32[512]{0:T(512)} copy(f32[512]{0:T(512)} %bitcast.8) | data formatting | bytes 4096
  111.4 0.0 copy-start
  111.4 2.9 %copy.26 = f32[100,4096]{1,0:T(8,128)} copy(f32[100,4096]{1,0:T(8,128)} %get-tuple-element.27) | data formatting | bytes 3276800
  114.3 0.0 copy-done
  114.3 0.0 copy-start.1
  114.3 1.2 %copy.27 = f32[100,4096]{1,0:T(8,128)} copy(f32[100,4096]{1,0:T(8,128)S(1)} %copy-done) | data formatting | bytes 3276800
  115.5 0.0 copy-done.1
  115.5 0.6 copy.28
Async XLA Ops:
  111.4 2.9 %copy-start = (f32[100,4096]{1,0:T(8,128)S(1)}, f32[100,4096]{1,0:T(8,128)}, u32[]{:S(2)}) copy-start(f32[100,4096]{1,0:T(8,128)} %get-tuple-element.28) | copy-start | bytes 4915204
  114.3 1.2 %copy-start.1 = (f32[1,4096]{1,0:T(1,128)S(1)}, f32[1,4096]{1,0:T(1,128)}, u32[]{:S(2)}) copy-start(f32[1,4096]{1,0:T(1,128)} %get-tuple-element.17) | copy-start | bytes 49156

commit v3 on v2

--- a/solution.py
+++ b/solution.py
@@ -14,6 +14,12 @@
 BF16 = jnp.bfloat16
 META = 16
 LANES = 128
+PIECE = 256
+
+
+def low_high(ids):
+    high = lax.div(ids, PIECE)
+    return ids - high * PIECE, high
 
 
 def split(x, n):
@@ -66,12 +72,12 @@
 
 def round_kernel(
     n_dom, n_dim,
-    ent_re_in, ent_im_in, ent_acc_in, rel_re_in, rel_im_in, rel_acc_in, lhs_in, rhs_in, ids_in, neg_in, bs_in,
-    new_re, new_im, new_acc, new_rre, new_rim, new_racc,
-    ent_re, ent_im, ent_acc, rel_re, rel_im, rel_acc, lhs_ref, rhs_ref, ids_ref, neg_ref, bs_ref,
+    ent_re_in, ent_im_in, rel_re_in, rel_im_in, lhs_in, rhs_in, ids_in, neg_in, bs_in,
+    gent_out, ent_sq, acc_out, rel_sq,
+    ent_re, ent_im, rel_re, rel_im, lhs_ref, rhs_ref, ids_ref, neg_ref, bs_ref,
     qs, qr, mt, mr, bf, bt, bp, wts, gqo, gqr, gbo, gbr, gent,
-    slots, acc, batch, esq, rsq,
-    in_sem,
+    slots, acc, batch, hot_ref, esq, rsq,
+    in_sem, out_sem,
     q_send, q_recv, m_send, m_recv, b_send, b_recv, g_send, g_recv, e_send, e_recv,
     send, recv, eq_send, eq_recv, rq_send, rq_recv,
 ):
@@ -131,7 +137,6 @@
     for k, (src, dst) in enumerate([
         (lhs_in, lhs_ref), (rhs_in, rhs_ref), (ids_in, ids_ref), (neg_in, neg_ref), (bs_in, bs_ref),
         (ent_re_in, ent_re), (ent_im_in, ent_im), (rel_re_in, rel_re), (rel_im_in, rel_im),
-        (ent_acc_in, ent_acc), (rel_acc_in, rel_acc),
     ]):
         fetches.append(pltpu.make_async_copy(src, dst, in_sem.at[k]))
         fetches[-1].start()
@@ -175,18 +180,19 @@
     h_re, h_im = pick(ent_re[...], hot_lhs, 3), pick(ent_im[...], hot_lhs, 3)
     for fetch in fetches[7:]:
         fetch.wait()
-    chunk = 512
+    base, high_of = low_high(ids)
+    hot_ids = one_hot(base, 0, PIECE)
 
     def gather(c, carry):
-        first = pl.multiple_of(c * chunk, chunk)
-        hot = one_hot(ids, first, chunk)
+        first = pl.multiple_of(c * PIECE, PIECE)
+        here = high_of == c
         return (
-            carry[0] + pick(rel_re[:, pl.ds(first, chunk)], hot, 3),
-            carry[1] + pick(rel_im[:, pl.ds(first, chunk)], hot, 3),
+            jnp.where(here, pick(rel_re[:, pl.ds(first, PIECE)], hot_ids, 3), carry[0]),
+            jnp.where(here, pick(rel_im[:, pl.ds(first, PIECE)], hot_ids, 3), carry[1]),
         )
 
     empty = jnp.zeros((width, edges), F32)
-    r_re, r_im = lax.fori_loop(0, rel_count // chunk, gather, (empty, empty))
+    r_re, r_im = lax.fori_loop(0, rel_count // PIECE, gather, (empty, empty))
     q_re = h_re * r_re - h_im * r_im
     q_im = h_re * r_im + h_im * r_re
     for g in range(groups):
@@ -333,6 +339,8 @@
         gent[...] += gbr[other(o)]
     gent[0:width, :] += put(gq_re * r_re + gq_im * r_im, hot_lhs, 2)
     gent[wp : wp + width, :] += put(gq_im * r_re - gq_re * r_im, hot_lhs, 2)
+    gent_copy = pltpu.make_async_copy(gent, gent_out, out_sem.at[0])
+    gent_copy.start()
     g_re, g_im = gent[0:width, :], gent[wp : wp + width, :]
     esq[d] = jnp.sum(g_re * g_re, 0, keepdims=True) + jnp.sum(g_im * g_im, 0, keepdims=True)
     for o in range(1, n_dim):
@@ -382,31 +390,34 @@
             cross(far)
 
     per_batch = batch.shape[1] // edges
-    piece = min(256, rel_count)
-    labels = lax.broadcasted_iota(jnp.int32, (piece, per_batch * edges), 0).astype(F32).astype(BF16)
+    lanes = lax.broadcasted_iota(jnp.int32, (edges, PIECE), 1)
 
     def add_up(js, fresh):
-        names = []
+        highs = []
         for k, j in enumerate(js):
             cut = slice(k * edges, (k + 1) * edges)
             high, low = split(slots[j].reshape(kp, edges), 2)
             batch[0:kp, cut] = high
             batch[kp : 2 * kp, cut] = low
-            names.append(slots[j, 0, width : width + 1, :])
-        names = jnp.concatenate(names, 1)
+            base, piece_of = low_high(slots[j, 0, width : width + 1, :].astype(jnp.int32))
+            down_rows = jnp.transpose(jnp.broadcast_to(base.astype(F32), (LANES, edges))).astype(jnp.int32)
+            wide = jnp.concatenate([down_rows] * (PIECE // LANES), 1)
+            hot_ref[cut, :] = jnp.where(lanes == wide, 1.0, 0.0).astype(BF16)
+            highs.append(piece_of)
+        highs = jnp.concatenate(highs, 1).astype(F32).astype(BF16)
 
         def body(c, carry):
-            first = pl.multiple_of(c * piece, piece)
-            mine = (names - first.astype(F32)).astype(BF16)
-            hot = jnp.where(labels == mine, jnp.ones((), BF16), jnp.zeros((), BF16))
-            both = lax.dot_general(batch[...], hot, turned, preferred_element_type=F32)
+            first = pl.multiple_of(c * PIECE, PIECE)
+            here = highs == c.astype(F32).astype(BF16)
+            mine = jnp.where(here, batch[...], jnp.zeros((), BF16))
+            both = jnp.dot(mine, hot_ref[...], preferred_element_type=F32)
             total = both[0:kp] + both[kp : 2 * kp]
             if not fresh:
-                total = total + acc[:, pl.ds(first, piece)]
-            acc[:, pl.ds(first, piece)] = total
+                total = total + acc[:, pl.ds(first, PIECE)]
+            acc[:, pl.ds(first, PIECE)] = total
             return carry
 
-        lax.fori_loop(0, rel_count // piece, body, 0)
+        lax.fori_loop(0, rel_count // PIECE, body, 0)
 
     add_up([index(zz, y, x) for zz in range(per_batch)], True)
     for lot in range(1, deep // per_batch):
@@ -416,11 +427,7 @@
     for o in range(1, n_dim):
         wait_for(esq.at[other(o)], eq_recv.at[other(o)])
         total = total + esq[other(o)]
-    total = ent_acc[...] + total / D
-    new_acc[...] = total
-    scale = RATE / jnp.sqrt(total)
-    new_re[...] = ent_re[...] - scale * gent[0:width, :]
-    new_im[...] = ent_im[...] - scale * gent[wp : wp + width, :]
+    ent_sq[...] = total
 
     for yy, xx, halves in ((y, 1 - x, (1,)), (1 - y, x, (0,)), (1 - y, 1 - x, (0, 1))):
 
@@ -434,6 +441,8 @@
 
         lax.fori_loop(0, deep // per_batch, rest, 0)
 
+    acc_copy = pltpu.make_async_copy(acc, acc_out, out_sem.at[1])
+    acc_copy.start()
     t_re, t_im = acc[0:width, :], acc[wp : wp + width, :]
     rsq[d] = jnp.sum(t_re * t_re, 0, keepdims=True) + jnp.sum(t_im * t_im, 0, keepdims=True)
     for o in range(1, n_dim):
@@ -442,11 +451,7 @@
     for o in range(1, n_dim):
         wait_for(rsq.at[other(o)], rq_recv.at[other(o)])
         total = total + rsq[other(o)]
-    total = rel_acc[...] + total / D
-    new_racc[...] = total
-    scale = RATE / jnp.sqrt(total)
-    new_rre[...] = rel_re[...] - scale * acc[0:width, :]
-    new_rim[...] = rel_im[...] - scale * acc[wp : wp + width, :]
+    rel_sq[...] = total
 
     def drain(zz, carry):
         j = index(zz, y, x)
@@ -467,6 +472,8 @@
         return carry
 
     lax.fori_loop(0, deep, drain, 0)
+    gent_copy.wait()
+    acc_copy.wait()
     for o in range(1, n_dim):
         wait_for(bf.at[d], b_send.at[o])
         wait_for(gbo.at[d], e_send.at[o])
@@ -480,6 +487,22 @@
         for o in range(1, n_dim):
             wait_for(qs.at[0], q_send.at[i, o])
             wait_for(gqo.at[i, 0], g_send.at[i, o])
+
+
+def update_kernel(
+    gent, ent_sq, ent_re, ent_im, ent_acc, acc, rel_sq, rel_re, rel_im, rel_acc,
+    new_re, new_im, new_acc, new_rre, new_rim, new_racc,
+):
+    width, wp = ent_re.shape[0], gent.shape[0] // 2
+    for grad, sq, old_re, old_im, old, out_re, out_im, out in (
+        (gent, ent_sq, ent_re, ent_im, ent_acc, new_re, new_im, new_acc),
+        (acc, rel_sq, rel_re, rel_im, rel_acc, new_rre, new_rim, new_racc),
+    ):
+        total = old[...] + sq[...] / D
+        out[...] = total
+        scale = RATE / jnp.sqrt(total)
+        out_re[...] = old_re[...] - scale * grad[0:width, :]
+        out_im[...] = old_im[...] - scale * grad[wp : wp + width, :]
 
 
 def per_device(
@@ -499,14 +522,16 @@
     dma = pltpu.SemaphoreType.DMA
     shape = jax.ShapeDtypeStruct
     args = (
-        ent_re, ent_im, ent_acc.reshape(1, rows), rel_re, rel_im, rel_acc.reshape(1, rel_count),
+        ent_re, ent_im, rel_re, rel_im,
         lhs_rows, rhs_rows, rel_ids, neg_rows, bucket_step.reshape(1, groups),
     )
-    outs = pl.pallas_call(
+    gent, ent_sq, acc, rel_sq = pl.pallas_call(
         functools.partial(round_kernel, n_dom, n_dim),
-        out_shape=tuple(shape(a.shape, F32) for a in args[:6]),
+        out_shape=(
+            shape((kp, rows), F32), shape((1, rows), F32), shape((kp, rel_count), F32), shape((1, rel_count), F32)
+        ),
         in_specs=[hbm] * len(args),
-        out_specs=(vmem,) * 6,
+        out_specs=(hbm, vmem, hbm, vmem),
         scratch_shapes=[pltpu.VMEM(a.shape, a.dtype) for a in args] + [
             pltpu.VMEM((groups, kp, per_edge), F32),
             pltpu.VMEM((units, n_dim, kp, per_edge), F32),
@@ -524,9 +549,10 @@
             pltpu.VMEM((n_dom, 2, wp, edges), F32),
             pltpu.VMEM((kp, rel_count), F32),
             pltpu.VMEM((2 * kp, 4 * edges), BF16),
+            pltpu.VMEM((4 * edges, PIECE), BF16),
             pltpu.VMEM((n_dim, 1, rows), F32),
             pltpu.VMEM((n_dim, 1, rel_count), F32),
-            dma((len(args),)),
+            dma((len(args),)), dma((2,)),
             dma((units, n_dim)), dma((units, n_dim)),
             dma((units,)), dma((units,)),
             dma((n_dim,)), dma((n_dim,)),
@@ -540,6 +566,26 @@
             collective_id=0, has_side_effects=True, vmem_limit_bytes=60 * 1024 * 1024
         ),
     )(*args)
+    steps = rows // LANES
+    ent, ent_row = pl.BlockSpec((width, LANES), lambda c: (0, c)), pl.BlockSpec((1, LANES), lambda c: (0, c))
+    some = rel_count // steps
+    rel, rel_row = pl.BlockSpec((width, some), lambda c: (0, c)), pl.BlockSpec((1, some), lambda c: (0, c))
+    outs = pl.pallas_call(
+        update_kernel,
+        grid=(steps,),
+        out_shape=tuple(shape(s, F32) for s in (
+            (width, rows), (width, rows), (1, rows), (width, rel_count), (width, rel_count), (1, rel_count)
+        )),
+        in_specs=[
+            pl.BlockSpec((kp, LANES), lambda c: (0, c)), ent_row, ent, ent, ent_row,
+            pl.BlockSpec((kp, some), lambda c: (0, c)), rel_row, rel, rel, rel_row,
+        ],
+        out_specs=(ent, ent, ent_row, rel, rel, rel_row),
+        compiler_params=pltpu.CompilerParams(vmem_limit_bytes=60 * 1024 * 1024),
+    )(
+        gent, ent_sq, ent_re, ent_im, ent_acc.reshape(1, rows),
+        acc, rel_sq, rel_re, rel_im, rel_acc.reshape(1, rel_count),
+    )
     return outs[0], outs[1], outs[2].reshape(rows), outs[3], outs[4], outs[5].reshape(rel_count)
 
 

time: 117 us -> 112 us (0.957)
  local copies, waits for them, and re-layouts: 9.21 us -> 0 us
  Pallas kernels: 106 us -> 111 us
    unnamed x10 -> x0, local copies, waits for them, and re-layouts: 9.21 us -> none
    pallas_call x1 -> x2, Pallas kernels: 106 us -> 111 us  [the longest x1 106 us: per_device(): pl.pallas_call(functools.partial(round_kernel, n_dom, n_dim), out_shape=(...]
where the time goes in v3:
time: 112 us
  Pallas kernels  111 us (99%)
    pallas_call x1, Pallas kernels, per_device(): pl.pallas_call(functools.partial(round_kernel, n_dom, n_dim), out_shape=(...  106 us
    pallas_call x1, Pallas kernels, per_device(): pl.pallas_call(update_kernel, grid=(steps,), out_shape=tuple((shape(s, F3...  5.57 us

profile of v3, /device:TPU:0, one launch (start us, length us, event | category | flops | bytes accessed | tf_op | source)
XLA Modules:
  0.0 112.1 jit_solution(9228794202662198236)
XLA Ops:
  0.6 105.9 %shard_map.154 = (f32[208,512]{1,0:T(8,128)}, f32[1,512]{1,0:T(1,128)}, f32[208,4096]{1,0:T(8,128)}, f32[1,4096]{1,0:T(1,128)}) custom-call(f32[100,512]{1,0:T(8,128)} %ent_re.1, f32[100,512]{1,0:T(8,128)} %ent_im.1, f32[100,4096]{1,0:T(8,128)} %rel_re.1, f32[100,4096]{1,0:T(8,128)} %rel_im.1, s32[2,128]{1,0:T(2,128)} %lhs_in.1, s32[2,128]{1,0:T(2,128)} %rhs_in.1, ...), custom_call_target="tpu_custom_call" | custom-call | tf_op jit(solution)/shard_map/pallas_call | solution.py:528
  106.5 5.6 %shard_map.155 = (f32[100,512]{1,0:T(8,128)}, f32[100,512]{1,0:T(8,128)}, f32[1,512]{1,0:T(1,128)}, f32[100,4096]{1,0:T(8,128)}, f32[100,4096]{1,0:T(8,128)}, /*index=5*/f32[1,4096]{1,0:T(1,128)}) custom-call(f32[208,512]{1,0:T(8,128)} %get-tuple-element.16.gent, f32[1,512]{1,0:T(1,128)} %get-tuple-element.17.ent_sq, f32[100,512]{1,0:T(8,128)} %ent_re.1, ...), custom_call_target="tpu_custom_call" | custom-call | tf_op jit(solution)/shard_map/pallas_call | solution.py:573

commit v4 on v3

--- a/solution.py
+++ b/solution.py
@@ -142,8 +142,7 @@
         fetches[-1].start()
     mt[...] = jnp.full(mt.shape, -1, jnp.int32)
     qs[...] = jnp.zeros(qs.shape, F32)
-    for half in (0, 1):
-        slots[p, half] = jnp.zeros((wp, edges), F32)
+    slots[p] = jnp.zeros((kp, edges), F32)
     bf[d] = jnp.zeros((kp, rows), F32)
     for fetch in fetches[:7]:
         fetch.wait()
@@ -298,40 +297,57 @@
         cols.append(total)
     gq = jnp.concatenate(cols, 1)
     gq_re, gq_im = gq[0:width], gq[wp : wp + width]
-    slots[p, 0, 0:width, :] = gq_re * h_re + gq_im * h_im
-    slots[p, 1, 0:width, :] = gq_im * h_re - gq_re * h_im
-    slots[p, 0, width : width + 1, :] = ids.astype(F32)
-
-    def pass_on(j, half, way, target):
-        remote(slots.at[j, half], slots.at[j, half], send.at[j, half, way], recv.at[j, half], (target, d)).start()
-
-    def arrived(j, half):
-        wait_for(slots.at[j, half], recv.at[j, half])
-
-    def sent(j, half, way):
-        wait_for(slots.at[j, half], send.at[j, half, way])
+    slots[p, 0:width, :] = gq_re * h_re + gq_im * h_im
+    slots[p, wp : wp + width, :] = gq_im * h_re - gq_re * h_im
+    slots[p, width : width + 1, :] = ids.astype(F32)
+
+    thin = max(1, (kp // 8 + 4) // 9) * 8
+    thick = (kp - 2 * thin) // 2
+    pieces = (pl.ds(0, thick), pl.ds(thick, thick), pl.ds(2 * thick, thin), pl.ds(2 * thick + thin, thin))
+    UP, DOWN, X, Y = range(4)
+    target = {UP: up, DOWN: down, X: to_x, Y: to_y}
+
+    def view(j, piece):
+        return slots.at[j, pieces[piece], :]
+
+    def pass_on(j, piece, way):
+        remote(
+            view(j, piece), view(j, piece), send.at[j, piece, way], recv.at[j, piece], (target[way], d)
+        ).start()
+
+    def arrived(j, piece):
+        wait_for(view(j, piece), recv.at[j, piece])
+
+    def sent(j, piece, way):
+        wait_for(view(j, piece), send.at[j, piece, way])
 
     def spread(j):
-        pass_on(j, 0, 2, to_x)
-        pass_on(j, 1, 3, to_y)
-        pass_on(j, 0, 3, to_y)
-        pass_on(j, 1, 2, to_x)
-
-    def go_up(j):
+        pass_on(j, 0, X)
+        pass_on(j, 1, Y)
+        pass_on(j, 0, Y)
+        pass_on(j, 1, X)
+
+    def go_up(j, which):
         @pl.when(has_up)
         def _():
-            pass_on(j, 0, 0, up)
-            pass_on(j, 1, 0, up)
-
-    def go_down(j):
+            for piece in which:
+                pass_on(j, piece, UP)
+
+    def go_down(j, which):
         @pl.when(has_down)
         def _():
-            pass_on(j, 0, 1, down)
-            pass_on(j, 1, 1, down)
-
-    go_up(p)
-    go_down(p)
+            for piece in which:
+                pass_on(j, piece, DOWN)
+
+    go_up(p, (0, 1))
+    go_down(p, (0, 1))
+    pass_on(p, 2, X)
+    pass_on(p, 3, Y)
     spread(p)
+    pass_on(p, 3, X)
+    pass_on(p, 2, Y)
+    go_up(p, (2, 3))
+    go_down(p, (2, 3))
 
     gent[...] = gbo[d]
     for o in range(1, n_dim):
@@ -346,60 +362,16 @@
     for o in range(1, n_dim):
         remote(esq.at[d], esq.at[d], eq_send.at[o], eq_recv.at[d], (p, other(o))).start()
 
-    def cross(zz):
-        from_x, from_y = index(zz, y, 1 - x), index(zz, 1 - y, x)
-        arrived(from_x, 0)
-        pass_on(from_x, 0, 3, to_y)
-        arrived(from_y, 1)
-        pass_on(from_y, 1, 2, to_x)
-
-    def column(k, carry):
-        below, above = z - k, z + k
-
-        @pl.when(below >= 0)
-        def _():
-            j = index(below, y, x)
-            arrived(j, 0)
-            arrived(j, 1)
-            go_up(j)
-            spread(j)
-
-        @pl.when(above < deep)
-        def _():
-            j = index(above, y, x)
-            arrived(j, 0)
-            arrived(j, 1)
-            go_down(j)
-            spread(j)
-
-        @pl.when(below + 1 >= 0)
-        def _():
-            cross(below + 1)
-
-        @pl.when((above - 1 < deep) & (k > 1))
-        def _():
-            cross(above - 1)
-
-        return carry
-
-    lax.fori_loop(1, deep, column, 0)
-    for far in (z - (deep - 1), z + (deep - 1)):
-
-        @pl.when((far >= 0) & (far < deep))
-        def _(far=far):
-            cross(far)
-
-    per_batch = batch.shape[1] // edges
     lanes = lax.broadcasted_iota(jnp.int32, (edges, PIECE), 1)
 
     def add_up(js, fresh):
         highs = []
         for k, j in enumerate(js):
             cut = slice(k * edges, (k + 1) * edges)
-            high, low = split(slots[j].reshape(kp, edges), 2)
+            high, low = split(slots[j], 2)
             batch[0:kp, cut] = high
             batch[kp : 2 * kp, cut] = low
-            base, piece_of = low_high(slots[j, 0, width : width + 1, :].astype(jnp.int32))
+            base, piece_of = low_high(slots[j, width : width + 1, :].astype(jnp.int32))
             down_rows = jnp.transpose(jnp.broadcast_to(base.astype(F32), (LANES, edges))).astype(jnp.int32)
             wide = jnp.concatenate([down_rows] * (PIECE // LANES), 1)
             hot_ref[cut, :] = jnp.where(lanes == wide, 1.0, 0.0).astype(BF16)
@@ -419,27 +391,129 @@
 
         lax.fori_loop(0, rel_count // PIECE, body, 0)
 
-    add_up([index(zz, y, x) for zz in range(per_batch)], True)
-    for lot in range(1, deep // per_batch):
-        add_up([index(lot * per_batch + zz, y, x) for zz in range(per_batch)], False)
+    def cross(zz):
+        from_x, from_y = index(zz, y, 1 - x), index(zz, 1 - y, x)
+        arrived(from_x, 0)
+        pass_on(from_x, 0, Y)
+        arrived(from_y, 1)
+        pass_on(from_y, 1, X)
+
+    def plane():
+        from_x, from_y, corner = index(z, y, 1 - x), index(z, 1 - y, x), index(z, 1 - y, 1 - x)
+        arrived(from_x, 2)
+        pass_on(from_x, 2, Y)
+        arrived(from_y, 3)
+        pass_on(from_y, 3, X)
+        go_up(from_x, (2,))
+        go_down(from_x, (2,))
+        go_up(from_y, (3,))
+        go_down(from_y, (3,))
+        for j, piece in ((from_x, 3), (from_y, 2), (corner, 2), (corner, 3)):
+            arrived(j, piece)
+            go_up(j, (piece,))
+            go_down(j, (piece,))
+
+    def planes(k):
+        below, above = z - k, z + k
+
+        @pl.when(below >= 0)
+        def _():
+            for q in range(4):
+                j = below * 4 + q
+                for piece in (2, 3):
+                    arrived(j, piece)
+                    go_up(j, (piece,))
+
+        @pl.when(above < deep)
+        def _():
+            for q in range(4):
+                j = above * 4 + q
+                for piece in (2, 3):
+                    arrived(j, piece)
+                    go_down(j, (piece,))
+
+    def add_plane(zz, fresh):
+        for yy, xx, which in ((y, 1 - x, (1,)), (1 - y, x, (0,)), (1 - y, 1 - x, (0, 1))):
+            for piece in which:
+                arrived(index(zz, yy, xx), piece)
+        add_up([zz * 4 + q for q in range(4)], fresh)
+
+    def add_planes(k):
+        below, above = z - k, z + k
+
+        @pl.when(below >= 0)
+        def _():
+            add_plane(below, False)
+
+        @pl.when(above < deep)
+        def _():
+            add_plane(above, False)
+
+    def column(k, carry):
+        below, above = z - k, z + k
+
+        @pl.when(below >= 0)
+        def _():
+            j = index(below, y, x)
+            arrived(j, 0)
+            arrived(j, 1)
+            go_up(j, (0, 1))
+            spread(j)
+
+        @pl.when(above < deep)
+        def _():
+            j = index(above, y, x)
+            arrived(j, 0)
+            arrived(j, 1)
+            go_down(j, (0, 1))
+            spread(j)
+
+        @pl.when(below + 1 >= 0)
+        def _():
+            cross(below + 1)
+
+        @pl.when((above - 1 < deep) & (k > 1))
+        def _():
+            cross(above - 1)
+
+        @pl.when(k == 1)
+        def _():
+            plane()
+
+        @pl.when(k > 1)
+        def _():
+            planes(k - 1)
+
+        @pl.when(k == 2)
+        def _():
+            add_plane(z, True)
+
+        @pl.when(k > 2)
+        def _():
+            add_planes(k - 2)
+
+        return carry
+
+    lax.fori_loop(1, deep, column, 0)
+    for far in (z - (deep - 1), z + (deep - 1)):
+
+        @pl.when((far >= 0) & (far < deep))
+        def _(far=far):
+            cross(far)
+
+    last = deep - 1
+    if deep == 2:
+        add_plane(z, True)
+    if deep > 2:
+        add_planes(last - 1)
+    planes(last)
+    add_planes(last)
 
     total = esq[d]
     for o in range(1, n_dim):
         wait_for(esq.at[other(o)], eq_recv.at[other(o)])
         total = total + esq[other(o)]
     ent_sq[...] = total
-
-    for yy, xx, halves in ((y, 1 - x, (1,)), (1 - y, x, (0,)), (1 - y, 1 - x, (0, 1))):
-
-        def rest(lot, carry, yy=yy, xx=xx, halves=halves):
-            js = [index(lot * per_batch + zz, yy, xx) for zz in range(per_batch)]
-            for j in js:
-                for half in halves:
-                    arrived(j, half)
-            add_up(js, False)
-            return carry
-
-        lax.fori_loop(0, deep // per_batch, rest, 0)
 
     acc_copy = pltpu.make_async_copy(acc, acc_out, out_sem.at[1])
     acc_copy.start()
@@ -455,22 +529,35 @@
 
     def drain(zz, carry):
         j = index(zz, y, x)
-        for half in (0, 1):
-
-            @pl.when((zz <= z) & has_up)
-            def _(half=half):
-                sent(j, half, 0)
-
-            @pl.when((zz >= z) & has_down)
-            def _(half=half):
-                sent(j, half, 1)
-
-            sent(j, half, 2)
-            sent(j, half, 3)
-        sent(index(zz, y, 1 - x), 0, 3)
-        sent(index(zz, 1 - y, x), 1, 2)
+
+        @pl.when((zz <= z) & has_up)
+        def _():
+            sent(j, 0, UP)
+            sent(j, 1, UP)
+            for q in range(4):
+                sent(zz * 4 + q, 2, UP)
+                sent(zz * 4 + q, 3, UP)
+
+        @pl.when((zz >= z) & has_down)
+        def _():
+            sent(j, 0, DOWN)
+            sent(j, 1, DOWN)
+            for q in range(4):
+                sent(zz * 4 + q, 2, DOWN)
+                sent(zz * 4 + q, 3, DOWN)
+
+        for piece in (0, 1):
+            sent(j, piece, X)
+            sent(j, piece, Y)
+        sent(index(zz, y, 1 - x), 0, Y)
+        sent(index(zz, 1 - y, x), 1, X)
         return carry
 
+    for piece in (2, 3):
+        sent(p, piece, X)
+        sent(p, piece, Y)
+    sent(index(z, y, 1 - x), 2, Y)
+    sent(index(z, 1 - y, x), 3, X)
     lax.fori_loop(0, deep, drain, 0)
     gent_copy.wait()
     acc_copy.wait()
@@ -546,7 +633,7 @@
             pltpu.VMEM((n_dim, kp, rows), F32),
             pltpu.VMEM((n_dim, kp, rows), F32),
             pltpu.VMEM((kp, rows), F32),
-            pltpu.VMEM((n_dom, 2, wp, edges), F32),
+            pltpu.VMEM((n_dom, kp, edges), F32),
             pltpu.VMEM((kp, rel_count), F32),
             pltpu.VMEM((2 * kp, 4 * edges), BF16),
             pltpu.VMEM((4 * edges, PIECE), BF16),
@@ -558,7 +645,7 @@
             dma((n_dim,)), dma((n_dim,)),
             dma((units, n_dim)), dma((STEPS, groups)),
             dma((n_dim,)), dma((n_dim,)),
-            dma((n_dom, 2, 4)), dma((n_dom, 2)),
+            dma((n_dom, 4, 4)), dma((n_dom, 4)),
             dma((n_dim,)), dma((n_dim,)),
             dma((n_dim,)), dma((n_dim,)),
         ],

time: 112 us -> 111 us (level)
    pallas_call x1, Pallas kernels: 106 us -> 104 us  [per_device(): pl.pallas_call(functools.partial(round_kernel, n_dom, n_dim), out_shape=(...]
where the time goes in v4:
time: 111 us
  Pallas kernels  110 us (99%)
    pallas_call x1, Pallas kernels, per_device(): pl.pallas_call(functools.partial(round_kernel, n_dom, n_dim), out_shape=(...  104 us
    pallas_call x1, Pallas kernels, per_device(): pl.pallas_call(update_kernel, grid=(steps,), out_shape=tuple((shape(s, F3...  5.57 us

profile of v4, /device:TPU:0, one launch (start us, length us, event | category | flops | bytes accessed | tf_op | source)
XLA Modules:
  0.0 110.6 jit_solution(5813820826844545228)
XLA Ops:
  0.6 104.3 %shard_map.154 = (f32[208,512]{1,0:T(8,128)}, f32[1,512]{1,0:T(1,128)}, f32[208,4096]{1,0:T(8,128)}, f32[1,4096]{1,0:T(1,128)}) custom-call(f32[100,512]{1,0:T(8,128)} %ent_re.1, f32[100,512]{1,0:T(8,128)} %ent_im.1, f32[100,4096]{1,0:T(8,128)} %rel_re.1, f32[100,4096]{1,0:T(8,128)} %rel_im.1, s32[2,128]{1,0:T(2,128)} %lhs_in.1, s32[2,128]{1,0:T(2,128)} %rhs_in.1, ...), custom_call_target="tpu_custom_call" | custom-call | tf_op jit(solution)/shard_map/pallas_call | solution.py:615
  104.9 5.6 %shard_map.155 = (f32[100,512]{1,0:T(8,128)}, f32[100,512]{1,0:T(8,128)}, f32[1,512]{1,0:T(1,128)}, f32[100,4096]{1,0:T(8,128)}, f32[100,4096]{1,0:T(8,128)}, /*index=5*/f32[1,4096]{1,0:T(1,128)}) custom-call(f32[208,512]{1,0:T(8,128)} %get-tuple-element.16.gent, f32[1,512]{1,0:T(1,128)} %get-tuple-element.17.ent_sq, f32[100,512]{1,0:T(8,128)} %ent_re.1, ...), custom_call_target="tpu_custom_call" | custom-call | tf_op jit(solution)/shard_map/pallas_call | solution.py:660

commit v5 on v4

--- a/solution.py
+++ b/solution.py
@@ -484,14 +484,6 @@
         def _():
             planes(k - 1)
 
-        @pl.when(k == 2)
-        def _():
-            add_plane(z, True)
-
-        @pl.when(k > 2)
-        def _():
-            add_planes(k - 2)
-
         return carry
 
     lax.fori_loop(1, deep, column, 0)
@@ -502,10 +494,13 @@
             cross(far)
 
     last = deep - 1
-    if deep == 2:
-        add_plane(z, True)
-    if deep > 2:
-        add_planes(last - 1)
+    add_plane(z, True)
+
+    def nearer(k, carry):
+        add_planes(k)
+        return carry
+
+    lax.fori_loop(1, last, nearer, 0)
     planes(last)
     add_planes(last)
 
@@ -653,8 +648,8 @@
             collective_id=0, has_side_effects=True, vmem_limit_bytes=60 * 1024 * 1024
         ),
     )(*args)
-    steps = rows // LANES
-    ent, ent_row = pl.BlockSpec((width, LANES), lambda c: (0, c)), pl.BlockSpec((1, LANES), lambda c: (0, c))
+    steps = 2 * (rows // LANES)
+    ent, ent_row = pl.BlockSpec((width, LANES), lambda c: (0, c // 2)), pl.BlockSpec((1, LANES), lambda c: (0, c // 2))
     some = rel_count // steps
     rel, rel_row = pl.BlockSpec((width, some), lambda c: (0, c)), pl.BlockSpec((1, some), lambda c: (0, c))
     outs = pl.pallas_call(
@@ -664,7 +659,7 @@
             (width, rows), (width, rows), (1, rows), (width, rel_count), (width, rel_count), (1, rel_count)
         )),
         in_specs=[
-            pl.BlockSpec((kp, LANES), lambda c: (0, c)), ent_row, ent, ent, ent_row,
+            pl.BlockSpec((kp, LANES), lambda c: (0, c // 2)), ent_row, ent, ent, ent_row,
             pl.BlockSpec((kp, some), lambda c: (0, c)), rel_row, rel, rel, rel_row,
         ],
         out_specs=(ent, ent, ent_row, rel, rel, rel_row),

time: 111 us -> 119 us (1.072)
  Pallas kernels: 110 us -> 118 us
    pallas_call x1, Pallas kernels: 104 us -> 111 us  [per_device(): pl.pallas_call(functools.partial(round_kernel, n_dom, n_dim), out_shape=(...]
    pallas_call x1, Pallas kernels: 5.57 us -> 7.59 us  [per_device(): pl.pallas_call(update_kernel, grid=(steps,), out_shape=tuple((shape(s, F3...]
where the time goes in v5:
time: 119 us
  Pallas kernels  118 us (99%)
    pallas_call x1, Pallas kernels, per_device(): pl.pallas_call(functools.partial(round_kernel, n_dom, n_dim), out_shape=(...  111 us
    pallas_call x1, Pallas kernels, per_device(): pl.pallas_call(update_kernel, grid=(steps,), out_shape=tuple((shape(s, F3...  7.59 us

profile of v5, /device:TPU:0, one launch (start us, length us, event | category | flops | bytes accessed | tf_op | source)
XLA Modules:
  0.0 119.0 jit_solution(5761793949070830933)
XLA Ops:
  0.6 110.8 %shard_map.154 = (f32[208,512]{1,0:T(8,128)}, f32[1,512]{1,0:T(1,128)}, f32[208,4096]{1,0:T(8,128)}, f32[1,4096]{1,0:T(1,128)}) custom-call(f32[100,512]{1,0:T(8,128)} %ent_re.1, f32[100,512]{1,0:T(8,128)} %ent_im.1, f32[100,4096]{1,0:T(8,128)} %rel_re.1, f32[100,4096]{1,0:T(8,128)} %rel_im.1, s32[2,128]{1,0:T(2,128)} %lhs_in.1, s32[2,128]{1,0:T(2,128)} %rhs_in.1, ...), custom_call_target="tpu_custom_call" | custom-call | tf_op jit(solution)/shard_map/pallas_call | solution.py:610
  111.4 7.6 %shard_map.155 = (f32[100,512]{1,0:T(8,128)}, f32[100,512]{1,0:T(8,128)}, f32[1,512]{1,0:T(1,128)}, f32[100,4096]{1,0:T(8,128)}, f32[100,4096]{1,0:T(8,128)}, /*index=5*/f32[1,4096]{1,0:T(1,128)}) custom-call(f32[208,512]{1,0:T(8,128)} %get-tuple-element.16.gent, f32[1,512]{1,0:T(1,128)} %get-tuple-element.17.ent_sq, f32[100,512]{1,0:T(8,128)} %ent_re.1, ...), custom_call_target="tpu_custom_call" | custom-call | tf_op jit(solution)/shard_map/pallas_call | solution.py:655
